TPU v7x, 128 devices: a whole 4x4x4 slice. The times are simulated.
128 devices in a mesh: occ: 32 (over x, y_lo, z), aux: 4 (over y_hi, core).
Axes of the slice: x: 4, y: 4 (y_hi: 2, y_lo: 2; y = y_hi * 2 + y_lo), z: 4, core: 2. Of those that a mesh axis runs over, the one named last changes fastest.
Arguments:
- b_aux: bfloat16 [8192, 64, 256], P(('occ', 'aux')), may hold values from -0.06982422 to 0.06982422
- eps_occ: float32 [64], replicated, may hold values from -3 to -0.3
- eps_vir: float32 [4096], replicated, may hold values from 0.5 to 3
- domains: int32 [64, 2], replicated, may hold values from 0 to 31
- pair_keep: int32 [64, 7], P('occ'), may hold values 0 or 1
Outputs:
- gamma: bfloat16 [8192, 64, 256], P(('occ', 'aux'))
All inputs are finite; a program needn't handle non-finite values. No bound on the sum of `pair_keep` on one device may be relied on, other than what follows from the above.
Results may differ from a plain program's by a relative error of at most 0.0042.
Values may be sent and summed in bfloat16 or wider, within the bound.
A program may use at most 128 MiB of HBM per device.

v0:
```python
import jax
import jax.numpy as jnp
from jax import lax
from jax.sharding import PartitionSpec as P

VBLK = 128
KMAX = 2
H = 3


def from_behind(value, axis, steps):
    count = lax.axis_size(axis)
    pairs = [(source, (source + steps) % count) for source in range(count)]
    return lax.ppermute(value, axis, pairs)


def amplitudes(coulomb, vir_rows, vir_part, occ_rows, occ_part):
    denom = (
        vir_rows[:, :, None, None]
        + vir_part[None, None, :, :]
        - occ_rows[:, None, None, None]
        - occ_part[None, None, :, None]
    )
    return -coulomb / denom


def step_ahead(block):
    return from_behind(block, "occ", 1)


def step_behind(block):
    return from_behind(block, "occ", -1)


def shards(b_aux, eps_occ, eps_vir, domains, pair_keep):
    mine = lax.all_to_all(b_aux, "occ", split_axis=1, concat_axis=0, tiled=True)
    n_batch = lax.axis_size("occ")
    me_batch = lax.axis_index("occ")
    per = mine.shape[1]
    keep = pair_keep.astype(jnp.bfloat16)
    offsets = jnp.arange(VBLK, dtype=jnp.int32)

    def batch_energies(batch):
        start = batch * per
        occ_part = lax.dynamic_slice_in_dim(eps_occ, start, per, 0)
        dom_part = lax.dynamic_slice_in_dim(domains, start, per, 0)
        index = (dom_part[:, :, None] * VBLK + offsets[None, None, :]).reshape(per, KMAX * VBLK)
        return (occ_part, eps_vir[index])

    occ_rows, vir_rows = batch_energies(me_batch)

    def pair_amps(partner, offset):
        occ_part, vir_part = batch_energies((me_batch - offset) % n_batch)
        partial_sum = jnp.einsum("pia,pjc->iajc", mine, partner, preferred_element_type=jnp.float32)
        coulomb = lax.psum(partial_sum, "aux")
        return amplitudes(coulomb, vir_rows, vir_part, occ_rows, occ_part).astype(jnp.bfloat16)

    def contract(total, rounded, offset, partner):
        weighted = rounded * keep[:, offset + H][:, None, None, None]
        return total + jnp.einsum(
            "iajc,pjc->pia", weighted, partner, preferred_element_type=jnp.float32
        )

    def pair_term(total, partner, offset):
        return contract(total, pair_amps(partner, offset), offset, partner)

    total = jnp.zeros(mine.shape, jnp.float32)
    total = pair_term(total, mine, 0)
    ahead = mine
    for step in range(1, H + 1):
        ahead = step_ahead(ahead)
        total = pair_term(total, ahead, step)
    behind = mine
    for step in range(1, H + 1):
        behind = step_behind(behind)
        total = pair_term(total, behind, -step)
    gamma_local = total.astype(jnp.bfloat16)
    return lax.all_to_all(gamma_local, "occ", split_axis=0, concat_axis=1, tiled=True)


def solution(mesh):
    in_specs = (P(("occ", "aux"), None, None), P(), P(), P(), P("occ", None))
    out_specs = P(("occ", "aux"), None, None)
    return jax.shard_map(shards, mesh=mesh, in_specs=in_specs, out_specs=out_specs, check_vma=False)
```

profile of v0, /device:TPU:1, one launch (start us, length us, event | category | flops | bytes accessed | tf_op | source)
XLA Modules:
  0.0 414.5 jit_solution(11993422382425338946)
XLA Ops:
  6.5 2.8 copy.62
  9.3 35.5 %all_to_all.36 = bf16[64,64,256]{2,0,1:T(8,128)(2,1)S(1)} all-to-all(bf16[64,64,256]{2,0,1:T(8,128)(2,1)S(1)} %copy.62), channel_id=1, replica_groups=mesh['occ'=32,'aux'=4] {'occ'}, dimensions={1} | all-to-all | bytes 4194304 | tf_op jit(solution)/shard_map/all_to_all | solution.py:36
  44.8 0.1 copy.63
  44.9 1.5 collective-permute-start
  46.4 4.2 %collective-permute-start.3 = (bf16[2048,2,256]{2,0,1:T(8,128)(2,1)S(1)}, bf16[2048,2,256]{2,0,1:T(8,128)(2,1)S(1)}, u32[]{:S(2)}, u32[]{:S(2)}) collective-permute-start(bf16[2048,2,256]{2,0,1:T(8,128)(2,1)S(1)} %bitcast.154), channel_id=1, source_target_pairs={{0,124},{4,0},{8,4},{12,8},{16,12},{20,16},{24,20},{28,24},{32,28}... | collective-permute-start | bytes 6291464 | tf_op jit(solution)/shard_map/ppermute | solution.py:14
  50.7 42.8 %collective-permute-done = bf16[2048,2,256]{2,0,1:T(8,128)(2,1)S(1)} collective-permute-done((bf16[2048,2,256]{2,0,1:T(8,128)(2,1)S(1)}, bf16[2048,2,256]{2,0,1:T(8,128)(2,1)S(1)}, u32[]{:S(2)}, u32[]{:S(2)}) %collective-permute-start) | collective-permute-done | bytes 2097184 | tf_op jit(solution)/shard_map/ppermute | solution.py:14
  93.6 5.7 %collective-permute-start.4 = (bf16[2048,2,256]{2,0,1:T(8,128)(2,1)S(1)}, bf16[2048,2,256]{2,0,1:T(8,128)(2,1)S(1)}, u32[]{:S(2)}, u32[]{:S(2)}) collective-permute-start(bf16[2048,2,256]{2,0,1:T(8,128)(2,1)S(1)} %collective-permute-done.3), channel_id=1, source_target_pairs={{0,124},{4,0},{8,4},{12,8},{16,12},{20,16},{24,20},{28,24},{32,28}... | collective-permute-start | bytes 6291464 | tf_op jit(solution)/shard_map/ppermute | solution.py:14
  99.2 41.9 %collective-permute-done.1 = bf16[2048,2,256]{2,0,1:T(8,128)(2,1)S(1)} collective-permute-done((bf16[2048,2,256]{2,0,1:T(8,128)(2,1)S(1)}, bf16[2048,2,256]{2,0,1:T(8,128)(2,1)S(1)}, u32[]{:S(2)}, u32[]{:S(2)}) %collective-permute-start.1) | collective-permute-done | bytes 2097184 | tf_op jit(solution)/shard_map/ppermute | solution.py:14
  141.2 5.7 %collective-permute-start.5 = (bf16[2048,2,256]{2,0,1:T(8,128)(2,1)S(1)}, bf16[2048,2,256]{2,0,1:T(8,128)(2,1)S(1)}, u32[]{:S(2)}, u32[]{:S(2)}) collective-permute-start(bf16[2048,2,256]{2,0,1:T(8,128)(2,1)S(1)} %collective-permute-done.4), channel_id=1, source_target_pairs={{0,124},{4,0},{8,4},{12,8},{16,12},{20,16},{24,20},{28,24},{32,28}... | collective-permute-start | bytes 6291464 | tf_op jit(solution)/shard_map/ppermute | solution.py:14
  146.8 2.3 fusion.28
  149.1 2.3 fusion.26
  151.4 2.2 fusion.14
  153.6 2.3 fusion.22
  155.9 2.3 fusion.10
  158.2 29.7 %collective-permute-done.2 = bf16[2048,2,256]{2,0,1:T(8,128)(2,1)S(1)} collective-permute-done((bf16[2048,2,256]{2,0,1:T(8,128)(2,1)S(1)}, bf16[2048,2,256]{2,0,1:T(8,128)(2,1)S(1)}, u32[]{:S(2)}, u32[]{:S(2)}) %collective-permute-start.2) | collective-permute-done | bytes 2097184 | tf_op jit(solution)/shard_map/ppermute | solution.py:14
  187.8 2.3 fusion.18
  190.1 1.3 copy-done.2
  191.4 2.3 fusion.6
  193.9 0.5 copy-done.22
  194.5 0.1 copy.77
  195.0 0.1 copy.69
  196.0 3.3 gather_fusion.7
  199.4 3.1 gather_fusion.1
  202.6 3.1 gather_fusion.2
  205.8 3.1 gather_fusion.3
  209.0 3.1 gather_fusion.4
  212.1 3.1 gather_fusion.5
  215.3 3.1 gather_fusion.6
  218.5 3.1 gather_fusion
  221.7 0.1 fusion.86
  221.8 0.2 slice_reduce_fusion
  222.0 120.7 %all-reduce.3.cloned.1.call-done = (f32[2,256,2,256]{3,1,2,0:T(8,128)}, f32[2,256,2,256]{3,1,2,0:T(8,128)}, f32[2,256,2,256]{3,1,2,0:T(8,128)}, f32[2,256,2,256]...) async-done(((f32[2,256,2,256]{3,1,2,0:T(8,128)}, f32[2,256,2,256]{3,1,2,0:T(8,128)}, ...) | async-done | bytes 7340048 | tf_op jit(solution)/shard_map/psum | solution.py:55
  342.8 2.8 fusion.45
  345.6 1.4 fusion.8
  347.0 0.1 copy-done.9
  347.2 0.3 copy-done.20
  347.4 1.4 fusion.12
  348.9 0.2 copy-done.11
  349.0 0.3 copy-done.19
  349.3 3.4 fusion.16
  352.7 3.4 fusion.20
  356.1 3.4 fusion.24
  359.5 7.0 %fusion.1 = bf16[2048,2,256]{0,2,1:T(8,128)(2,1)} fusion(f32[2,256,2048,1]{2,1,3,0:T(8,128)S(1)} %fusion.8, f32[2,256,2048,1]{2,1,3,0:T(8,128)S(1)} %fusion.12, f32[2,256,2048,1]{2,1,3,0:T(8,128)} %fusion.16, f32[2,256,2048,1]{2,1,3,0:T(8,128)} %fusion.20, f32[2,256,2048,1]{2,1,3,0:T(8,128)} %fusion.24, f32[2,256,2048,1]{2,1,3,0:T(8,128)S(1)} %fusion.45, ...), kind=kOutput, calls=%fused_computation.15 | convolution fusion | flops 1082916864 | bytes 30412820 | tf_op jit(solution)/shard_map/iajc,pjc->pia/dot_general | solution.py:60
  366.5 4.8 %copy.78 = bf16[2048,2,256]{2,1,0:T(2,128)(2,1)S(1)} copy(bf16[2048,2,256]{0,2,1:T(8,128)(2,1)} %fusion.1) | data formatting | bytes 4194304 | tf_op jit(solution)/shard_map/convert_element_type | solution.py:77
  371.4 33.4 %all_to_all.37 = bf16[2048,2,256]{2,1,0:T(2,128)(2,1)S(1)} all-to-all(bf16[2048,2,256]{2,1,0:T(2,128)(2,1)S(1)} %copy.78), channel_id=1, replica_groups=mesh['occ'=32,'aux'=4] {'occ'}, dimensions={0} | all-to-all | bytes 4194304 | tf_op jit(solution)/shard_map/all_to_all | solution.py:78
  404.7 0.3 copy.79
  405.0 0.1 copy.80
  405.2 2.5 copy.81
  (97 shorter events, 1.7 us)
Async XLA Ops:
  6.5 189.5 %copy-start = (f32[4096]{0:T(1024)S(1)}, f32[4096]{0:T(1024)}, u32[]{:S(2)}) copy-start(f32[4096]{0:T(1024)} %param.7) | copy-start | bytes 49156
  6.5 336.2 %all-reduce.3.cloned.1.call-start = ((), (), s32[]{:S(2)}) async-start(), calls=%async_computation.2 | async-start | bytes 14680064 | tf_op jit(solution)/shard_map/psum | solution.py:55
  44.9 48.6 %collective-permute-start = (bf16[2048,2,256]{2,0,1:T(8,128)(2,1)S(1)}, bf16[2048,2,256]{2,0,1:T(8,128)(2,1)S(1)}, u32[]{:S(2)}, u32[]{:S(2)}) collective-permute-start(bf16[2048,2,256]{2,0,1:T(8,128)(2,1)S(1)} %bitcast.153), channel_id=1, source_target_pairs={{0,4},{4,8},{8,12},{12,16},{16,20},{20,24},{24,28},{28,32},{32,36}... | collective-permute-start | bytes 6291464 | tf_op jit(solution)/shard_map/ppermute | solution.py:14
  46.4 47.1 %collective-permute-start.3 = (bf16[2048,2,256]{2,0,1:T(8,128)(2,1)S(1)}, bf16[2048,2,256]{2,0,1:T(8,128)(2,1)S(1)}, u32[]{:S(2)}, u32[]{:S(2)}) collective-permute-start(bf16[2048,2,256]{2,0,1:T(8,128)(2,1)S(1)} %bitcast.154), channel_id=1, source_target_pairs={{0,124},{4,0},{8,4},{12,8},{16,12},{20,16},{24,20},{28,24},{32,28}... | collective-permute-start | bytes 6291464 | tf_op jit(solution)/shard_map/ppermute | solution.py:14
  93.5 55.6 %copy-start.4 = (bf16[2048,2,256]{2,0,1:T(8,128)(2,1)}, bf16[2048,2,256]{2,0,1:T(8,128)(2,1)S(1)}, u32[]{:S(2)}) copy-start(bf16[2048,2,256]{2,0,1:T(8,128)(2,1)S(1)} %collective-permute-done) | copy-start | bytes 6291460
  93.5 47.6 %collective-permute-start.1 = (bf16[2048,2,256]{2,0,1:T(8,128)(2,1)S(1)}, bf16[2048,2,256]{2,0,1:T(8,128)(2,1)S(1)}, u32[]{:S(2)}, u32[]{:S(2)}) collective-permute-start(bf16[2048,2,256]{2,0,1:T(8,128)(2,1)S(1)} %collective-permute-done), channel_id=1, source_target_pairs={{0,4},{4,8},{8,12},{12,16},{16,20},{20,24},{24,28},{28,32},{32,36}... | collective-permute-start | bytes 6291464 | tf_op jit(solution)/shard_map/ppermute | solution.py:14
  93.5 57.8 %copy-start.8 = (bf16[2048,2,256]{2,0,1:T(8,128)(2,1)}, bf16[2048,2,256]{2,0,1:T(8,128)(2,1)S(1)}, u32[]{:S(2)}) copy-start(bf16[2048,2,256]{2,0,1:T(8,128)(2,1)S(1)} %collective-permute-done.3) | copy-start | bytes 6291460
  93.6 47.6 %collective-permute-start.4 = (bf16[2048,2,256]{2,0,1:T(8,128)(2,1)S(1)}, bf16[2048,2,256]{2,0,1:T(8,128)(2,1)S(1)}, u32[]{:S(2)}, u32[]{:S(2)}) collective-permute-start(bf16[2048,2,256]{2,0,1:T(8,128)(2,1)S(1)} %collective-permute-done.3), channel_id=1, source_target_pairs={{0,124},{4,0},{8,4},{12,8},{16,12},{20,16},{24,20},{28,24},{32,28}... | collective-permute-start | bytes 6291464 | tf_op jit(solution)/shard_map/ppermute | solution.py:14
  141.1 12.5 %copy-start.6 = (bf16[2048,2,256]{2,0,1:T(8,128)(2,1)}, bf16[2048,2,256]{2,0,1:T(8,128)(2,1)S(1)}, u32[]{:S(2)}) copy-start(bf16[2048,2,256]{2,0,1:T(8,128)(2,1)S(1)} %collective-permute-done.1) | copy-start | bytes 6291460
  141.1 46.7 %collective-permute-start.2 = (bf16[2048,2,256]{2,0,1:T(8,128)(2,1)S(1)}, bf16[2048,2,256]{2,0,1:T(8,128)(2,1)S(1)}, u32[]{:S(2)}, u32[]{:S(2)}) collective-permute-start(bf16[2048,2,256]{2,0,1:T(8,128)(2,1)S(1)} %collective-permute-done.1), channel_id=1, source_target_pairs={{0,4},{4,8},{8,12},{12,16},{16,20},{20,24},{24,28},{28,32},{32,36}... | collective-permute-start | bytes 6291464 | tf_op jit(solution)/shard_map/ppermute | solution.py:14
  141.2 14.7 %copy-start.12 = (bf16[2048,2,256]{2,0,1:T(8,128)(2,1)}, bf16[2048,2,256]{2,0,1:T(8,128)(2,1)S(1)}, u32[]{:S(2)}) copy-start(bf16[2048,2,256]{2,0,1:T(8,128)(2,1)S(1)} %collective-permute-done.4) | copy-start | bytes 6291460
  141.2 48.9 %collective-permute-start.5 = (bf16[2048,2,256]{2,0,1:T(8,128)(2,1)S(1)}, bf16[2048,2,256]{2,0,1:T(8,128)(2,1)S(1)}, u32[]{:S(2)}, u32[]{:S(2)}) collective-permute-start(bf16[2048,2,256]{2,0,1:T(8,128)(2,1)S(1)} %collective-permute-done.4), channel_id=1, source_target_pairs={{0,124},{4,0},{8,4},{12,8},{16,12},{20,16},{24,20},{28,24},{32,28}... | collective-permute-start | bytes 6291464 | tf_op jit(solution)/shard_map/ppermute | solution.py:14
  187.8 2.3 copy-start.10
  190.1 1.3 copy-start.2
  193.7 0.7 copy-start.22
  193.7 0.7 copy-start.15
  215.3 6.4 %copy-start.16 = (f32[64]{0:T(128)S(1)}, f32[64]{0:T(128)}, u32[]{:S(2)}) copy-start(f32[64]{0:T(128)} %param.6) | copy-start | bytes 772
  342.8 2.8 copy-start.13
  342.8 2.8 copy-start.21
  345.6 1.6 copy-start.9
  345.6 1.8 copy-start.20
  347.4 1.6 copy-start.11
  347.4 1.9 copy-start.19
  349.3 3.4 copy-start.7
  349.3 3.4 copy-start.18
  352.7 3.4 copy-start.5
  352.7 3.4 copy-start.17
  356.1 3.4 copy-start.3
  356.1 3.4 copy-start.14
  405.2 2.5 copy-start.1
Sparse Core Ops, SparseCore 0:
  193.9 148.8 all-reduce.2
where the time goes:
time: 415 us
  waiting for transfers between devices  235 us (57%)
  blocking collectives  68.9 us (17%)
  local copies, waits for them, and re-layouts  40.6 us (10%)
  matrix products  38.7 us (9%)
  starting transfers between devices  17.1 us (4%)
  between operations  13.9 us (3%)
    psum x1, waiting for transfers between devices, pair_amps(): coulomb = lax.psum(partial_sum, 'aux')  121 us
    ppermute x6, waiting for transfers between devices, from_behind(): return lax.ppermute(value, axis, pairs)  114 us
    all_to_all x1, blocking collectives, shards(): mine = lax.all_to_all(b_aux, 'occ', split_axis=1, concat_axis=0, tiled=True)  35.5 us
    all_to_all x1, blocking collectives, shards(): lax.all_to_all(gamma_local, 'occ', split_axis=0, concat_axis=1, tiled=True)  33.4 us
    gather x16, local copies, waits for them, and re-layouts, batch_energies(): return (occ_part, eps_vir[index])  25.4 us
    dot_general x7, matrix products, contract(): jnp.einsum('iajc,pjc->pia', weighted, partner, preferred_element_type=jnp...  22.8 us
    ppermute x6, starting transfers between devices, from_behind(): return lax.ppermute(value, axis, pairs)  17.1 us
    dot_general x7, matrix products, pair_amps(): jnp.einsum('pia,pjc->iajc', mine, partner, preferred_element_type=jnp.flo...  15.9 us
  transfers between devices with their start and end apart: 7, of which 4 were waited for; matrix products, arithmetic and copies ran while one was open for 10% of the time, Pallas kernels for 0%

commit v1 on v0

v1 whole, which is shorter than its diff:
```python
import jax
import jax.numpy as jnp
from jax import lax
from jax.experimental import pallas as pl
from jax.experimental.pallas import tpu as pltpu
from jax.sharding import PartitionSpec as P

MESH = pl.DeviceIdType.MESH
F32 = jnp.float32
BF16 = jnp.bfloat16

PB = 64
W = 512
NB = 32
OWN = 4
HALO = 3
LOC = OWN + HALO
NCODE = 8
PS = NCODE * PB
WIN = OWN * W
COLS = ((0, 640), (640, 640), (1280, 768))
RS_DTYPES = (BF16, F32, F32)


def side(pos):
    return lax.rem(lax.div(pos + 1, 2), 2)


def kernel(b_ref, evir_ref, eocc_ref, dom_ref, keep_ref, out_ref,
           b3, bg, bt, acc, s0, r0, s1, r1, s2, r2, s3, r3, mb, mm, gam, go, rr, kb, erow, ecol,
           loc_sem, a_send, a_recv, c_send, c_recv, rs_send, rs_recv, ag_send, ag_recv,
           gc_send, gc_recv, o_send, o_recv, k_send, k_recv):
    occ = lax.axis_index("occ")
    aux = lax.axis_index("aux")
    core = lax.rem(aux, 2)
    pos = (lax.div(occ, 8), lax.div(aux, 2) * 2 + lax.rem(lax.div(occ, 4), 2), lax.rem(occ, 4))
    half = tuple(lax.div(p, 2) for p in pos)
    fs = tuple(side(p) for p in pos)
    code = fs[0] * 4 + fs[1] * 2 + fs[2]

    def device(x, y, z, c):
        return (x * 8 + lax.rem(y, 2) * 4 + z, lax.div(y, 2) * 2 + c)

    group_peers = []
    for r in range(1, 8):
        bits = ((r >> 2) & 1, (r >> 1) & 1, r & 1)
        where = [p + 1 - 2 * lax.rem(p, 2) if bit else p for p, bit in zip(pos, bits)]
        flips = [1 - f if bit else f for f, bit in zip(fs, bits)]
        group_peers.append((device(*where, core), flips[0] * 4 + flips[1] * 2 + flips[2]))
    slice_peers = []
    for d in range(3):
        where = list(pos)
        where[d] = 3 - pos[d]
        slice_peers.append(device(*where, core))
    sibling = device(*pos, 1 - core)

    def remote(src, dst, send, recv, dev):
        return pltpu.make_async_remote_copy(
            src_ref=src, dst_ref=dst, send_sem=send, recv_sem=recv, device_id=dev, device_id_type=MESH)

    loads = [pltpu.make_async_copy(b_ref.at[:, o], b3.at[:, :, pl.ds(o * 256, 256)], loc_sem.at[o]) for o in range(2)]
    for cp in loads:
        cp.start()
    kslot = kb.at[half[2], half[0], code]
    kcopy = pltpu.make_async_copy(keep_ref, kslot, loc_sem.at[2])
    kcopy.start()

    barrier = pltpu.get_barrier_semaphore()
    everyone = [dev for dev, _ in group_peers] + slice_peers + [sibling]
    for dev in everyone:
        pl.semaphore_signal(barrier, inc=1, device_id=dev, device_id_type=MESH)
    for cp in loads:
        cp.wait()
    kcopy.wait()
    pl.semaphore_wait(barrier, len(everyone))

    first = code * OWN - HALO + NB

    def send_in(t, _):
        for dev, q in group_peers:
            batch = lax.rem(q * OWN - HALO + NB + t, NB)
            remote(b3.at[batch], bg.at[t, pl.ds(pl.multiple_of(code * PB, PB), PB)], a_send.at[0], a_recv.at[t], dev).start()
        return 0

    lax.fori_loop(0, LOC, send_in, 0)
    for dev, q in group_peers:
        remote(kslot, kslot, k_send.at[0], k_recv.at[0], dev).start()

    def own_rows(t, _):
        batch = lax.rem(first + t, NB)
        bg[t, pl.ds(pl.multiple_of(code * PB, PB), PB), :] = b3[batch]
        return 0

    lax.fori_loop(0, LOC, own_rows, 0)

    for t in range(LOC):
        for o in range(2):
            orb = lax.rem(first + t, NB) * 2 + o
            for k in range(2):
                row = evir_ref[dom_ref[orb, k]] - eocc_ref[orb]
                lane = t * W + o * 256 + k * 128
                erow[:, lane:lane + 128] = row
                if t >= HALO:
                    at = lane - HALO * W
                    ecol[at:at + 128, :] = jnp.broadcast_to(row, (128, 128)).T

    def keep_group():
        pltpu.make_async_copy(kb.at[0, 0, pl.ds(0, 7)], kb.at[0, 0, pl.ds(0, 7)], k_recv.at[0]).wait()
        pltpu.make_async_copy(kb.at[0, 0, pl.ds(0, 7)], kb.at[0, 0, pl.ds(0, 7)], k_send.at[0]).wait()

    def keep_x():
        ref = kb.at[half[2], half[0]]
        return remote(ref, ref, k_send.at[1], k_recv.at[1], slice_peers[0])

    def keep_z():
        ref = kb.at[half[2]]
        return remote(ref, ref, k_send.at[2], k_recv.at[2], slice_peers[2])

    def orders(u):
        return [(u + n) % 3 for n in range(3)]

    def band(ref, c, rows, size, u):
        lo, width = COLS[u]
        return ref.at[c, pl.ds(rows, size), pl.ds(lo, width)]

    def wait_in(t):
        pltpu.make_async_copy(bg.at[0, pl.ds(0, 7 * PB)], bg.at[0, pl.ds(0, 7 * PB)], a_recv.at[t]).wait()

    def core_copy(c):
        return remote(s0.at[c % 2], r0.at[c], c_send.at[c], c_recv.at[c], sibling)

    rs_bufs = ((s1, r1), (s2, r2), (s3, r3))

    def rs_copy(n, c, u):
        size = 128 >> n
        sb, rb = rs_bufs[n]
        return remote(band(sb, c % 2, 0, size, u), band(rb, c, 0, size, u),
                      rs_send.at[n, c, u], rs_recv.at[n, c, u], slice_peers[orders(u)[n]])

    def base_rows(u, n):
        at = core * 0
        for m in range(n):
            at = at + half[orders(u)[m]] * (128 >> m)
        return at

    def ag_copy(n, c, u):
        size = 128 >> n
        rows = pl.multiple_of(core * 256 + base_rows(u, n + 1), 32)
        ref = band(mb, c, rows, size, u)
        return remote(ref, ref, ag_send.at[n, c, u], ag_recv.at[n, c, u], slice_peers[orders(u)[n]])

    def gc_copy(c):
        ref = mb.at[c, pl.ds(pl.multiple_of(core * 256, 256), 256)]
        return remote(ref, ref, gc_send.at[c], gc_recv.at[c], sibling)

    def stage_v(c):
        top = HALO + c
        if c == 0:
            for t in range(HALO):
                wait_in(t)
        wait_in(top)
        if c >= 2:
            core_copy(c - 2).wait_send()
        for h in range(2):
            lanes = core * 256 if h == 0 else (1 - core) * 256
            bt[h] = bg[top, :, pl.ds(pl.multiple_of(lanes, 256), 256)].T

        def offset(s, _):
            at = pl.ds(pl.multiple_of(s * W, W), W)
            other = bg[top - s]
            s0[c % 2, :, at] = jnp.dot(bt[1], other, preferred_element_type=F32)
            acc[c, :, at] = jnp.dot(bt[0], other, preferred_element_type=F32)
            return 0

        lax.fori_loop(0, OWN, offset, 0)
        core_copy(c).start()

    def fold(src, send_to, n, c, u):
        size = 128 >> n
        lo, width = COLS[u]
        cols = slice(lo, lo + width)
        d = orders(u)[n]
        base = base_rows(u, n)
        keep_at = half[d] * size
        send_at = (1 - half[d]) * size
        step = 32

        def body(k, _):
            near = pl.ds(pl.multiple_of(send_at + k * step, step), step)
            mine = pl.ds(pl.multiple_of(base + send_at + k * step, step), step)
            val = acc[c, mine, cols] + src[c, near, cols].astype(F32)
            send_to[c % 2, pl.ds(pl.multiple_of(k * step, step), step), cols] = val.astype(send_to.dtype)
            return 0

        lax.fori_loop(0, size // step, body, 0)
        rs_copy(n, c, u).start()

        def body2(k, _):
            near = pl.ds(pl.multiple_of(keep_at + k * step, step), step)
            mine = pl.ds(pl.multiple_of(base + keep_at + k * step, step), step)
            acc[c, mine, cols] = acc[c, mine, cols] + src[c, near, cols].astype(F32)
            return 0

        lax.fori_loop(0, size // step, body2, 0)

    def stage_rs(n, c):
        if n == 0:
            core_copy(c).wait_recv()
        for u in range(3):
            if n > 0:
                rs_copy(n - 1, c, u).wait_recv()
            if c >= 2:
                rs_copy(n, c - 2, u).wait_send()
            fold(r0 if n == 0 else rs_bufs[n - 1][1], rs_bufs[n][0], n, c, u)

    def stage_amp(c):
        for u in range(3):
            rs_copy(2, c, u).wait_recv()
            lo, width = COLS[u]
            base = pl.multiple_of(base_rows(u, 3), 32)
            rows = ecol[pl.ds(pl.multiple_of(c * W + core * 256 + base, 32), 32), :]
            for k in range(width // 128):
                at = lo + k * 128
                s, lane = at // W, at % W
                total = acc[c, pl.ds(base, 32), at:at + 128] + r3[c, 0:32, at:at + 128]
                src = (HALO + c - s) * W + lane
                denom = rows + erow[:, src:src + 128]
                mb[c, pl.ds(pl.multiple_of(core * 256 + base, 32), 32), at:at + 128] = (-total / denom).astype(BF16)
            ag_copy(2, c, u).start()

    def stage_ag(n, c):
        for u in range(3):
            ag_copy(n + 1, c, u).wait_recv()
            ag_copy(n, c, u).start()

    def stage_gc(c):
        for u in range(3):
            ag_copy(0, c, u).wait_recv()
        gc_copy(c).start()

    def flag(batch, orbital, offset):
        y = half[1] * 2 + lax.rem(lax.div(batch, 4), 2)
        x, z = lax.div(batch, 8), lax.rem(batch, 4)
        q = side(x) * 4 + side(y) * 2 + side(z)
        row = orbital * LOC + offset
        line = kb[lax.div(z, 2), lax.div(x, 2), q, row:row + 1, :]
        return jnp.broadcast_to(line, (256, 128)).astype(BF16)

    def finish(t):
        go[t] = gam[t].astype(BF16)
        rr[code, t] = go[t, pl.ds(pl.multiple_of(code * PB, PB), PB)]
        for dev, q in group_peers:
            remote(go.at[t, pl.ds(pl.multiple_of(q * PB, PB), PB)], rr.at[code, t], o_send.at[0], o_recv.at[t], dev).start()

    def nt(a, b):
        return lax.dot_general(a, b, (((1,), (1,)), ((), ())), preferred_element_type=F32)

    def stage_gamma(c):
        top = HALO + c
        gc_copy(c).wait_recv()
        batch = lax.rem(first + top, NB)
        for s in range(1, OWN):
            other = lax.rem(first + top - s, NB)
            for o in range(2):
                m = flag(other, o, HALO - s)
                for k in range(2):
                    lanes = slice(s * W + o * 256 + k * 128, s * W + o * 256 + k * 128 + 128)
                    for h in range(2):
                        mm[h * 256:h * 256 + 256, lanes] = mb[c, h * 256:h * 256 + 256, lanes] * m
        for s in range(OWN - 1, 0, -1):
            t = top - s
            part = jnp.dot(bg[top], mm[:, s * W:s * W + W], preferred_element_type=F32)
            if c == 0 and t < HALO:
                gam[t] = part
            else:
                gam[t] = gam[t] + part
            if s == OWN - 1:
                finish(t)
            elif c == OWN - 1:
                finish(t)
        for s in range(OWN):
            for h in range(2):
                m = flag(batch, h, HALO + s)
                for k in range(4):
                    lanes = slice(s * W + k * 128, s * W + k * 128 + 128)
                    mm[h * 256:h * 256 + 256, lanes] = mb[c, h * 256:h * 256 + 256, lanes] * m
        part = nt(bg[top], mm[:, 0:W])
        for s in range(1, OWN):
            part = part + nt(bg[top - s], mm[:, s * W:s * W + W])
        gam[top] = part
        if c == OWN - 1:
            finish(top)

    stages = [
        stage_v,
        lambda c: stage_rs(0, c),
        lambda c: stage_rs(1, c),
        lambda c: stage_rs(2, c),
        stage_amp,
        lambda c: stage_ag(1, c),
        lambda c: stage_ag(0, c),
        stage_gc,
        stage_gamma,
    ]
    for tick in range(len(stages) + OWN - 1):
        for c in range(OWN):
            n = tick - c
            if 0 <= n < len(stages):
                stages[n](c)
        if tick == 0:
            keep_group()
            keep_x().start()
        if tick == 2:
            keep_x().wait()
            keep_z().start()
        if tick == 4:
            keep_z().wait()

    pltpu.make_async_copy(rr.at[pl.ds(0, 7)], rr.at[pl.ds(0, 7)], a_send.at[0]).wait()
    for c in range(OWN):
        if c >= 2:
            core_copy(c).wait_send()
        gc_copy(c).wait_send()
        for u in range(3):
            for n in range(3):
                if c >= 2:
                    rs_copy(n, c, u).wait_send()
                ag_copy(n, c, u).wait_send()

    for t in range(LOC):
        pltpu.make_async_copy(bg.at[0, pl.ds(0, 7 * PB)], bg.at[0, pl.ds(0, 7 * PB)], o_recv.at[t]).wait()

    def combine(g, _):
        nxt = lax.rem(g + 1, NCODE)
        b3[g * OWN] = rr[g, HALO]
        for k in range(1, OWN):
            b3[g * OWN + k] = (rr[g, HALO + k].astype(F32) + rr[nxt, k - 1].astype(F32)).astype(BF16)
        return 0

    lax.fori_loop(0, NCODE, combine, 0)
    stores = [pltpu.make_async_copy(b3.at[:, :, pl.ds(o * 256, 256)], out_ref.at[:, o], loc_sem.at[o]) for o in range(2)]
    for cp in stores:
        cp.start()
    for cp in stores:
        cp.wait()
    pltpu.make_async_copy(rr.at[pl.ds(0, 7)], rr.at[pl.ds(0, 7)], o_send.at[0]).wait()


def shards(b_aux, eps_occ, eps_vir, domains, pair_keep):
    rows = jnp.transpose(b_aux, (1, 0, 2)).reshape(NB, 2, PB, 256)
    keep = jnp.broadcast_to(pair_keep.astype(F32).reshape(2 * LOC, 1), (2 * LOC, 128))
    keep = jnp.pad(keep, ((0, 2), (0, 0)))
    dma, vm = pltpu.SemaphoreType.DMA, pltpu.VMEM
    hbm = pl.BlockSpec(memory_space=pl.ANY)
    vmem = pl.BlockSpec(memory_space=pltpu.VMEM)
    smem = pl.BlockSpec(memory_space=pltpu.SMEM)
    rs1, rs2, rs3 = RS_DTYPES
    out = pl.pallas_call(
        kernel,
        out_shape=jax.ShapeDtypeStruct((NB, 2, PB, 256), BF16),
        in_specs=[hbm, vmem, smem, smem, hbm],
        out_specs=hbm,
        scratch_shapes=[
            vm((NB, PB, W), BF16),
            vm((LOC, PS, W), BF16),
            vm((2, 256, PS), BF16),
            vm((OWN, 256, WIN), F32),
            vm((2, 256, WIN), F32), vm((OWN, 256, WIN), F32),
            vm((2, 128, WIN), rs1), vm((OWN, 128, WIN), rs1),
            vm((2, 64, WIN), rs2), vm((OWN, 64, WIN), rs2),
            vm((2, 32, WIN), rs3), vm((OWN, 32, WIN), rs3),
            vm((OWN, W, WIN), BF16),
            vm((W, WIN), BF16),
            vm((LOC, PS, W), F32),
            vm((LOC, PS, W), BF16),
            vm((NCODE, LOC, PB, W), BF16),
            vm((2, 2, NCODE, 16, 128), F32),
            vm((1, LOC * W), F32),
            vm((OWN * W, 128), F32),
            dma((3,)), dma((1,)), dma((LOC,)),
            dma((OWN,)), dma((OWN,)),
            dma((3, OWN, 3)), dma((3, OWN, 3)),
            dma((3, OWN, 3)), dma((3, OWN, 3)),
            dma((OWN,)), dma((OWN,)),
            dma((1,)), dma((LOC,)),
            dma((3,)), dma((3,)),
        ],
        compiler_params=pltpu.CompilerParams(
            collective_id=0, has_side_effects=True, vmem_limit_bytes=62 * 1024 * 1024),
    )(rows, eps_vir.reshape(32, 1, 128), eps_occ, domains, keep)
    return jnp.transpose(out.reshape(2 * NB, PB, 256), (1, 0, 2))


def solution(mesh):
    in_specs = (P(("occ", "aux"), None, None), P(), P(), P(), P("occ", None))
    out_specs = P(("occ", "aux"), None, None)
    return jax.shard_map(shards, mesh=mesh, in_specs=in_specs, out_specs=out_specs, check_vma=False)
```

time: 415 us -> 167 us (0.40)
  waiting for transfers between devices: 235 us -> 0 us
  Pallas kernels: 0 us -> 155 us
  blocking collectives: 68.9 us -> 0 us
  matrix products: 38.7 us -> 0 us
  local copies, waits for them, and re-layouts: 40.6 us -> 10.3 us
  starting transfers between devices: 17.1 us -> 0 us
  between operations: 13.9 us -> 0.01 us
    pallas_call x0 -> x1, Pallas kernels: none -> 155 us  [shards(): pl.pallas_call(kernel, out_shape=jax.ShapeDtypeStruct((NB, 2, PB, 256), B...]
    psum x1 -> x0, waiting for transfers between devices: 121 us -> none  [pair_amps(): coulomb = lax.psum(partial_sum, 'aux')]
    ppermute x6 -> x0, waiting for transfers between devices: 114 us -> none  [from_behind(): return lax.ppermute(value, axis, pairs)]
    all_to_all x2 -> x0, blocking collectives: 68.9 us -> none  [the longest x1 35.5 us: shards(): mine = lax.all_to_all(b_aux, 'occ', split_axis=1, concat_axis=0, tiled=True)]
    dot_general x14 -> x0, matrix products: 38.7 us -> none  [the longest x7 22.8 us: contract(): jnp.einsum('iajc,pjc->pia', weighted, partner, preferred_element_type=jnp...]
    gather x16 -> x0, local copies, waits for them, and re-layouts: 25.4 us -> none  [batch_energies(): return (occ_part, eps_vir[index])]
    ppermute x6 -> x0, starting transfers between devices: 17.1 us -> none  [from_behind(): return lax.ppermute(value, axis, pairs)]
    convert_element_type x1 -> x0, local copies, waits for them, and re-layouts: 4.82 us -> none  [shards(): gamma_local = total.astype(jnp.bfloat16)]
  transfers between devices with their start and end apart: 7 -> 0, of which waited for: 4 -> 0; matrix products, arithmetic and copies ran while one was open for 10% -> 0% of each run, Pallas kernels for 0% -> 0%
where the time goes in v1:
time: 167 us; the launch traced here: 166 us
  Pallas kernels  155 us (93%)
  local copies, waits for them, and re-layouts  10.3 us (6%)
    pallas_call x1, Pallas kernels, shards(): pl.pallas_call(kernel, out_shape=jax.ShapeDtypeStruct((NB, 2, PB, 256), B...  155 us
    reshape x1, local copies, waits for them, and re-layouts, shards(): return jnp.transpose(out.reshape(2 * NB, PB, 256), (1, 0, 2))  4.08 us
    transpose x1, local copies, waits for them, and re-layouts, shards(): rows = jnp.transpose(b_aux, (1, 0, 2)).reshape(NB, 2, PB, 256)  4.08 us

profile of v1, /device:TPU:1, one launch (start us, length us, event | category | flops | bytes accessed | tf_op | source)
XLA Modules:
  0.0 166.5 jit_solution(12480742459554399341)
XLA Ops:
  0.0 0.7 convert_element_type.5
  0.7 0.1 broadcast_in_dim.2
  0.8 0.7 pad.7.keep_ref
  1.4 1.4 copy.7.dom_ref
  2.8 4.1 %copy.6 = bf16[64,64,256]{2,1,0:T(8,128)(2,1)} copy(bf16[64,64,256]{2,0,1:T(8,128)(2,1)} %bitcast.9) | data formatting | bytes 4194304 | tf_op jit(solution)/shard_map/transpose | solution.py:350
  6.9 155.5 %shard_map.55 = bf16[32,2,64,256]{3,2,1,0:T(8,128)(2,1)} custom-call(bf16[32,2,64,256]{3,2,1,0:T(8,128)(2,1)} %bitcast.8, f32[32,1,128]{2,1,0:T(1,128)} %bitcast.10, f32[64]{0:T(128)} %eocc_ref.1, s32[64,2]{1,0:T(8,128)} %copy.7.dom_ref, f32[16,128]{1,0:T(8,128)} %pad.7.keep_ref), custom_call_target="tpu_custom_call" | custom-call | tf_op jit(solution)/shard_map/pallas_call | solution.py:358
  162.4 4.1 %copy.10 = bf16[64,64,256]{2,0,1:T(8,128)(2,1)} copy(bf16[64,64,256]{2,1,0:T(8,128)(2,1)} %bitcast.7) | data formatting | bytes 4194304 | tf_op jit(solution)/shard_map/reshape | solution.py:391
  (1 shorter events, 0.0 us)

commit v2 on v1

v2 whole, which is shorter than its diff:
```python
import functools

import jax
import jax.numpy as jnp
from jax import lax
from jax.experimental import pallas as pl
from jax.experimental.pallas import tpu as pltpu
from jax.sharding import PartitionSpec as P

MESH = pl.DeviceIdType.MESH
F32 = jnp.float32
BF16 = jnp.bfloat16

PB = 64
W = 512
NB = 32
OWN = 4
HALO = 3
LOC = OWN + HALO
NCODE = 8
PS = NCODE * PB
SLOTS = 4
ARRIVALS = (3, 4, 1, 0, 2, 5, 6)
UNITS = (
    (3, 1), (4, 2), (3, 3), (5, 1), (6, 2), (3, 0), (4, 1), (5, 2),
    (3, 2), (6, 3), (4, 0), (5, 3), (4, 3), (6, 0), (5, 0), (6, 1),
)
STEPS = (
    (0, 5), (1, 5), (0, 6), (0, 10), (1, 6), (2, 5), (1, 10), (0, 8), (0, 12), (1, 8), (2, 6), (1, 12),
    (2, 10), (3, 5), (0, 2), (3, 6), (1, 2), (4, 5), (2, 8), (2, 12), (3, 10), (4, 6), (0, 0), (5, 5),
    (0, 1), (3, 8), (3, 12), (1, 0), (2, 2), (4, 10), (1, 1), (5, 6), (6, 5), (4, 8), (0, 3), (4, 12),
    (0, 7), (0, 11), (0, 14), (2, 0), (1, 3), (1, 7), (2, 1), (3, 2), (1, 11), (5, 10), (6, 6), (1, 14),
    (7, 5), (5, 8), (5, 12), (0, 4), (8, 5), (3, 0), (3, 1), (1, 4), (2, 3), (2, 7), (2, 11), (4, 2),
    (7, 6), (0, 9), (6, 10), (6, 12), (8, 6), (6, 8), (1, 9), (4, 1), (2, 14), (2, 4), (3, 11), (4, 0),
    (3, 3), (5, 2), (3, 7), (7, 12), (0, 13), (8, 12), (7, 10), (0, 15), (7, 8), (1, 13), (2, 9), (8, 10),
    (5, 1), (3, 4), (4, 11), (1, 15), (5, 0), (8, 8), (4, 3), (3, 14), (6, 2), (4, 7), (6, 1), (2, 13),
    (4, 4), (5, 3), (3, 9), (5, 11), (6, 0), (2, 15), (7, 2), (5, 7), (4, 14), (5, 4), (8, 2), (6, 11),
    (3, 13), (4, 9), (7, 1), (6, 7), (8, 1), (7, 0), (6, 3), (6, 4), (3, 15), (4, 13), (8, 0), (5, 14),
    (7, 11), (5, 9), (8, 11), (7, 7), (4, 15), (7, 3), (5, 13), (8, 7), (7, 4), (8, 3), (6, 14), (6, 9),
    (8, 4), (5, 15), (6, 13), (7, 14), (7, 9), (6, 15), (8, 14), (8, 9), (7, 13), (8, 13), (7, 15), (8, 15),
)
RS_DTYPES = (BF16, BF16, F32)


def side(pos):
    return lax.rem(lax.div(pos + 1, 2), 2)


def kernel(steps, arrivals, units, b_ref, evir_ref, eocc_ref, dom_ref, keep_ref, out_ref,
           b3, bg, bt, acc, s0, r0, s1, r1, s2, r2, s3, r3, mb, mm, gam, go, rr, kb, erow, ecol,
           loc_sem, out_sem, a_send, a_recv, c_send, c_recv, rs_send, rs_recv, ag_send, ag_recv,
           gc_send, gc_recv, o_send, o_recv, k_send, k_recv):
    occ = lax.axis_index("occ")
    aux = lax.axis_index("aux")
    core = lax.rem(aux, 2)
    pos = (lax.div(occ, 8), lax.div(aux, 2) * 2 + lax.rem(lax.div(occ, 4), 2), lax.rem(occ, 4))
    half = tuple(lax.div(p, 2) for p in pos)
    fs = tuple(side(p) for p in pos)
    code = fs[0] * 4 + fs[1] * 2 + fs[2]

    def device(x, y, z, c):
        return (x * 8 + lax.rem(y, 2) * 4 + z, lax.div(y, 2) * 2 + c)

    group_peers = []
    for r in range(1, 8):
        bits = ((r >> 2) & 1, (r >> 1) & 1, r & 1)
        where = [p + 1 - 2 * lax.rem(p, 2) if bit else p for p, bit in zip(pos, bits)]
        flips = [1 - f if bit else f for f, bit in zip(fs, bits)]
        group_peers.append((device(*where, core), flips[0] * 4 + flips[1] * 2 + flips[2]))
    slice_peers = []
    for d in range(3):
        where = list(pos)
        where[d] = 3 - pos[d]
        slice_peers.append(device(*where, core))
    sibling = device(*pos, 1 - core)

    def remote(src, dst, send, recv, dev):
        return pltpu.make_async_remote_copy(
            src_ref=src, dst_ref=dst, send_sem=send, recv_sem=recv, device_id=dev, device_id_type=MESH)

    loads = [pltpu.make_async_copy(b_ref.at[:, o], b3.at[:, :, pl.ds(o * 256, 256)], loc_sem.at[o]) for o in range(2)]
    for cp in loads:
        cp.start()
    kslot = kb.at[half[2], half[0], code]
    for o in range(2):
        for k in range(LOC):
            kslot[o * LOC + k:o * LOC + k + 1, :] = jnp.full((1, 128), keep_ref[k, o].astype(F32))

    barrier = pltpu.get_barrier_semaphore()
    everyone = [dev for dev, _ in group_peers] + slice_peers + [sibling]
    for dev in everyone:
        pl.semaphore_signal(barrier, inc=1, device_id=dev, device_id_type=MESH)
    for cp in loads:
        cp.wait()
    pl.semaphore_wait(barrier, len(everyone))

    first = code * OWN - HALO + NB

    def send_in(t):
        for dev, q in group_peers:
            batch = lax.rem(q * OWN - HALO + NB + t, NB)
            remote(b3.at[batch], bg.at[t, pl.ds(pl.multiple_of(code * PB, PB), PB)], a_send.at[0], a_recv.at[t], dev).start()

    for t in arrivals:
        send_in(t)
    for dev, q in group_peers:
        remote(kslot, kslot, k_send.at[0], k_recv.at[0], dev).start()

    def own_rows(t, _):
        batch = lax.rem(first + t, NB)
        bg[t, pl.ds(pl.multiple_of(code * PB, PB), PB), :] = b3[batch]
        return 0

    lax.fori_loop(0, LOC, own_rows, 0)

    for t in range(LOC):
        for o in range(2):
            orb = lax.rem(first + t, NB) * 2 + o
            for k in range(2):
                row = evir_ref[dom_ref[k, orb]] - eocc_ref[orb]
                lane = t * W + o * 256 + k * 128
                erow[:, lane:lane + 128] = row
                if t >= HALO:
                    at = lane - HALO * W
                    ecol[at:at + 128, :] = jnp.broadcast_to(row, (128, 128)).T

    def keep_group():
        pltpu.make_async_copy(kb.at[0, 0, pl.ds(0, 7)], kb.at[0, 0, pl.ds(0, 7)], k_recv.at[0]).wait()
        pltpu.make_async_copy(kb.at[0, 0, pl.ds(0, 7)], kb.at[0, 0, pl.ds(0, 7)], k_send.at[0]).wait()

    def keep_x():
        ref = kb.at[half[2], half[0]]
        return remote(ref, ref, k_send.at[1], k_recv.at[1], slice_peers[0])

    def keep_z():
        ref = kb.at[half[2]]
        return remote(ref, ref, k_send.at[2], k_recv.at[2], slice_peers[2])

    def order(u, n):
        return (u + n) % 3

    def wait_in(t):
        pltpu.make_async_copy(bg.at[0, pl.ds(0, 7 * PB)], bg.at[0, pl.ds(0, 7 * PB)], a_recv.at[t]).wait()

    arrived, turned, touched = set(), set(), set()
    started = []
    left = [0] * LOC
    for top, s in units:
        left[top] += 1
        if s:
            left[top - s] += 1

    def core_copy(u):
        return remote(s0.at[started.index(u) % SLOTS], r0.at[u], c_send.at[u], c_recv.at[u], sibling)

    rs_bufs = ((s1, r1), (s2, r2), (s3, r3))

    def rs_copy(n, u):
        sb, rb = rs_bufs[n]
        return remote(sb.at[u], rb.at[u], rs_send.at[n, u], rs_recv.at[n, u], slice_peers[order(u, n)])

    def base_rows(u, n):
        at = core * 0
        for m in range(n):
            at = at + half[order(u, m)] * (128 >> m)
        return at

    def ag_copy(n, u):
        size = 128 >> n
        ref = mb.at[u, pl.ds(pl.multiple_of(core * 256 + base_rows(u, n + 1), 32), size)]
        return remote(ref, ref, ag_send.at[n, u], ag_recv.at[n, u], slice_peers[order(u, n)])

    def gc_copy(u):
        ref = mb.at[u, pl.ds(pl.multiple_of(core * 256, 256), 256)]
        return remote(ref, ref, gc_send.at[u], gc_recv.at[u], sibling)

    def stage_v(u):
        top, s = units[u]
        for t in (top, top - s):
            if t not in arrived:
                wait_in(t)
                arrived.add(t)
        own = top - HALO
        if top not in turned:
            turned.add(top)
            for h in range(2):
                lanes = core * 256 if h == 0 else (1 - core) * 256
                bt[own, h] = bg[top, :, pl.ds(pl.multiple_of(lanes, 256), 256)].T
        if len(started) >= SLOTS:
            core_copy(started[-SLOTS]).wait_send()
        started.append(u)
        other = bg[top - s]
        s0[started.index(u) % SLOTS] = jnp.dot(bt[own, 1], other, preferred_element_type=F32)
        core_copy(u).start()
        acc[u] = jnp.dot(bt[own, 0], other, preferred_element_type=F32)

    def fold(n, u):
        src = r0 if n == 0 else rs_bufs[n - 1][1]
        if n == 0:
            core_copy(u).wait_recv()
        else:
            rs_copy(n - 1, u).wait_recv()
        size = 128 >> n
        near_half = half[order(u, n)]
        base = base_rows(u, n)
        keep_at = near_half * size
        send_at = (1 - near_half) * size
        send_to = rs_bufs[n][0]
        step = 32

        def far(k, _):
            near = pl.ds(pl.multiple_of(send_at + k * step, step), step)
            mine = pl.ds(pl.multiple_of(base + send_at + k * step, step), step)
            val = acc[u, mine, :] + src[u, near, :].astype(F32)
            send_to[u, pl.ds(pl.multiple_of(k * step, step), step), :] = val.astype(send_to.dtype)
            return 0

        lax.fori_loop(0, size // step, far, 0)
        rs_copy(n, u).start()

        def stay(k, _):
            near = pl.ds(pl.multiple_of(keep_at + k * step, step), step)
            mine = pl.ds(pl.multiple_of(base + keep_at + k * step, step), step)
            acc[u, mine, :] = acc[u, mine, :] + src[u, near, :].astype(F32)
            return 0

        lax.fori_loop(0, size // step, stay, 0)

    def stage_amp(u):
        rs_copy(2, u).wait_recv()
        top, s = units[u]
        base = pl.multiple_of(base_rows(u, 3), 32)
        rows = ecol[pl.ds(pl.multiple_of((top - HALO) * W + core * 256 + base, 32), 32), :]
        for k in range(W // 128):
            lanes = slice(k * 128, k * 128 + 128)
            at = (top - s) * W + k * 128
            total = acc[u, pl.ds(base, 32), lanes] + r3[u, :, lanes]
            denom = rows + erow[:, at:at + 128]
            mb[u, pl.ds(pl.multiple_of(core * 256 + base, 32), 32), lanes] = (-total / denom).astype(BF16)
        ag_copy(2, u).start()

    def stage_ag(n, u):
        ag_copy(n + 1, u).wait_recv()
        ag_copy(n, u).start()

    def stage_gc(u):
        ag_copy(0, u).wait_recv()
        gc_copy(u).start()

    def flag(t, orbital, offset):
        batch = lax.rem(first + t, NB)
        y = half[1] * 2 + lax.rem(lax.div(batch, 4), 2)
        x, z = lax.div(batch, 8), lax.rem(batch, 4)
        q = side(x) * 4 + side(y) * 2 + side(z)
        row = orbital * LOC + offset
        line = kb[lax.div(z, 2), lax.div(x, 2), q, row:row + 1, :]
        return jnp.broadcast_to(line, (256, 128)).astype(BF16)

    finished = []

    def finish(t):
        finished.append(t)
        go[t] = gam[t].astype(BF16)
        for dev, q in group_peers:
            remote(go.at[t, pl.ds(pl.multiple_of(q * PB, PB), PB)], rr.at[code, t], o_send.at[0], o_recv.at[t], dev).start()
        rr[code, t] = go[t, pl.ds(pl.multiple_of(code * PB, PB), PB)]

    def add_term(t, part):
        if t in touched:
            gam[t] = gam[t] + part
        else:
            touched.add(t)
            gam[t] = part
        left[t] -= 1
        if left[t] == 0:
            finish(t)

    def stage_gamma(u):
        top, s = units[u]
        gc_copy(u).wait_recv()
        if s:
            for o in range(2):
                m = flag(top - s, o, HALO - s)
                for k in range(2):
                    lanes = slice(o * 256 + k * 128, o * 256 + k * 128 + 128)
                    for h in range(2):
                        mm[0, h * 256:h * 256 + 256, lanes] = mb[u, h * 256:h * 256 + 256, lanes] * m
            add_term(top - s, jnp.dot(bg[top], mm[0], preferred_element_type=F32))
        for h in range(2):
            m = flag(top, h, HALO + s)
            for k in range(4):
                lanes = slice(k * 128, k * 128 + 128)
                mm[1, h * 256:h * 256 + 256, lanes] = mb[u, h * 256:h * 256 + 256, lanes] * m
        add_term(top, lax.dot_general(bg[top - s], mm[1], (((1,), (1,)), ((), ())), preferred_element_type=F32))

    stages = [
        stage_v,
        lambda u: fold(0, u),
        lambda u: fold(1, u),
        lambda u: fold(2, u),
        stage_amp,
        lambda u: stage_ag(1, u),
        lambda u: stage_ag(0, u),
        stage_gc,
        stage_gamma,
    ]
    seen = set()
    for stage, u in steps:
        if stage not in seen:
            if stage == 1:
                keep_group()
                keep_x().start()
            if stage == 4:
                keep_x().wait()
                keep_z().start()
            if stage == 8:
                keep_z().wait()
        seen.add(stage)
        stages[stage](u)

    pltpu.make_async_copy(rr.at[pl.ds(0, 7)], rr.at[pl.ds(0, 7)], a_send.at[0]).wait()
    for at, u in enumerate(started):
        if at >= len(started) - SLOTS:
            core_copy(u).wait_send()
        gc_copy(u).wait_send()
        for n in range(3):
            rs_copy(n, u).wait_send()
            ag_copy(n, u).wait_send()

    got, done = set(), set()
    stores = []
    for t in finished:
        pltpu.make_async_copy(bg.at[0, pl.ds(0, 7 * PB)], bg.at[0, pl.ds(0, 7 * PB)], o_recv.at[t]).wait()
        got.add(t)
        for k in range(OWN):
            if k in done or HALO + k not in got or (k and k - 1 not in got):
                continue
            done.add(k)
            if k:
                def combine(g, _, k=k):
                    nxt = lax.rem(g + 1, NCODE)
                    rr[g, HALO + k] = (rr[g, HALO + k].astype(F32) + rr[nxt, k - 1].astype(F32)).astype(BF16)
                    return 0

                lax.fori_loop(0, NCODE, combine, 0)
            for o in range(2):
                cp = pltpu.make_async_copy(rr.at[:, HALO + k, :, pl.ds(o * 256, 256)], out_ref.at[:, k, o], out_sem.at[k, o])
                cp.start()
                stores.append(cp)
    for cp in stores:
        cp.wait()
    pltpu.make_async_copy(rr.at[pl.ds(0, 7)], rr.at[pl.ds(0, 7)], o_send.at[0]).wait()


def shards(b_aux, eps_occ, eps_vir, domains, pair_keep):
    rows = jnp.transpose(b_aux, (1, 0, 2)).reshape(NB, 2, PB, 256)
    dma, vm = pltpu.SemaphoreType.DMA, pltpu.VMEM
    hbm = pl.BlockSpec(memory_space=pl.ANY)
    vmem = pl.BlockSpec(memory_space=pltpu.VMEM)
    smem = pl.BlockSpec(memory_space=pltpu.SMEM)
    rs1, rs2, rs3 = RS_DTYPES
    n = len(UNITS)
    out = pl.pallas_call(
        functools.partial(kernel, STEPS, ARRIVALS, UNITS),
        out_shape=jax.ShapeDtypeStruct((NCODE, OWN, 2, PB, 256), BF16),
        in_specs=[hbm, vmem, smem, smem, smem],
        out_specs=hbm,
        scratch_shapes=[
            vm((NB, PB, W), BF16),
            vm((LOC, PS, W), BF16),
            vm((OWN, 2, 256, PS), BF16),
            vm((n, 256, W), F32),
            vm((SLOTS, 256, W), F32), vm((n, 256, W), F32),
            vm((n, 128, W), rs1), vm((n, 128, W), rs1),
            vm((n, 64, W), rs2), vm((n, 64, W), rs2),
            vm((n, 32, W), rs3), vm((n, 32, W), rs3),
            vm((n, W, W), BF16),
            vm((2, W, W), BF16),
            vm((LOC, PS, W), F32),
            vm((LOC, PS, W), BF16),
            vm((NCODE, LOC, PB, W), BF16),
            vm((2, 2, NCODE, 16, 128), F32),
            vm((1, LOC * W), F32),
            vm((OWN * W, 128), F32),
            dma((2,)), dma((OWN, 2)), dma((1,)), dma((LOC,)),
            dma((n,)), dma((n,)),
            dma((3, n)), dma((3, n)),
            dma((3, n)), dma((3, n)),
            dma((n,)), dma((n,)),
            dma((1,)), dma((LOC,)),
            dma((3,)), dma((3,)),
        ],
        compiler_params=pltpu.CompilerParams(
            collective_id=0, has_side_effects=True, vmem_limit_bytes=62 * 1024 * 1024),
    )(rows, eps_vir.reshape(32, 1, 128), eps_occ, domains.T, pair_keep.T)
    return jnp.transpose(out.reshape(2 * NB, PB, 256), (1, 0, 2))


def solution(mesh):
    in_specs = (P(("occ", "aux"), None, None), P(), P(), P(), P("occ", None))
    out_specs = P(("occ", "aux"), None, None)
    return jax.shard_map(shards, mesh=mesh, in_specs=in_specs, out_specs=out_specs, check_vma=False)
```

time: 167 us -> 156 us (0.934)
  Pallas kernels: 155 us -> 147 us
    pallas_call x1, Pallas kernels: 155 us -> 147 us  [shards(): pl.pallas_call(functools.partial(kernel, STEPS, ARRIVALS, UNITS), out_sha...]
where the time goes in v2:
time: 156 us
  Pallas kernels  147 us (94%)
  local copies, waits for them, and re-layouts  9.52 us (6%)
    pallas_call x1, Pallas kernels, shards(): pl.pallas_call(functools.partial(kernel, STEPS, ARRIVALS, UNITS), out_sha...  147 us
    reshape x1, local copies, waits for them, and re-layouts, shards(): return jnp.transpose(out.reshape(2 * NB, PB, 256), (1, 0, 2))  4.08 us
    transpose x1, local copies, waits for them, and re-layouts, shards(): rows = jnp.transpose(b_aux, (1, 0, 2)).reshape(NB, 2, PB, 256)  4.08 us

profile of v2, /device:TPU:1, one launch (start us, length us, event | category | flops | bytes accessed | tf_op | source)
XLA Modules:
  0.0 156.1 jit_solution(12735493127121203956)
XLA Ops:
  0.0 1.4 copy.7
  1.4 4.1 %copy.6 = bf16[64,64,256]{2,1,0:T(8,128)(2,1)} copy(bf16[64,64,256]{2,0,1:T(8,128)(2,1)} %bitcast.11) | data formatting | bytes 4194304 | tf_op jit(solution)/shard_map/transpose | solution.py:356
  5.4 146.6 %shard_map.55 = bf16[8,4,2,64,256]{4,3,2,1,0:T(8,128)(2,1)} custom-call(bf16[32,2,64,256]{3,2,1,0:T(8,128)(2,1)} %bitcast.10, f32[32,1,128]{2,1,0:T(1,128)} %bitcast.12, f32[64]{0:T(128)} %eocc_ref.1, s32[2,64]{1,0:T(2,128)} %bitcast.14, s32[7,2]{1,0:T(8,128)} %bitcast.13), custom_call_target="tpu_custom_call" | custom-call | tf_op jit(solution)/shard_map/pallas_call | solution.py:363
  152.1 4.1 %copy.10 = bf16[64,64,256]{2,0,1:T(8,128)(2,1)} copy(bf16[64,64,256]{2,1,0:T(8,128)(2,1)} %bitcast.9) | data formatting | bytes 4194304 | tf_op jit(solution)/shard_map/reshape | solution.py:396

commit v3 on v2

--- a/solution.py
+++ b/solution.py
@@ -20,26 +20,26 @@
 NCODE = 8
 PS = NCODE * PB
 SLOTS = 4
-ARRIVALS = (3, 4, 1, 0, 2, 5, 6)
+ARRIVALS = (4, 1, 3, 0, 2, 5, 6)
 UNITS = (
-    (3, 1), (4, 2), (3, 3), (5, 1), (6, 2), (3, 0), (4, 1), (5, 2),
-    (3, 2), (6, 3), (4, 0), (5, 3), (4, 3), (6, 0), (5, 0), (6, 1),
+    (3, 3), (3, 1), (4, 2), (6, 3), (5, 0), (4, 3), (5, 3), (5, 1),
+    (5, 2), (3, 0), (6, 1), (4, 1), (4, 0), (3, 2), (6, 0), (6, 2),
 )
 STEPS = (
-    (0, 5), (1, 5), (0, 6), (0, 10), (1, 6), (2, 5), (1, 10), (0, 8), (0, 12), (1, 8), (2, 6), (1, 12),
-    (2, 10), (3, 5), (0, 2), (3, 6), (1, 2), (4, 5), (2, 8), (2, 12), (3, 10), (4, 6), (0, 0), (5, 5),
-    (0, 1), (3, 8), (3, 12), (1, 0), (2, 2), (4, 10), (1, 1), (5, 6), (6, 5), (4, 8), (0, 3), (4, 12),
-    (0, 7), (0, 11), (0, 14), (2, 0), (1, 3), (1, 7), (2, 1), (3, 2), (1, 11), (5, 10), (6, 6), (1, 14),
-    (7, 5), (5, 8), (5, 12), (0, 4), (8, 5), (3, 0), (3, 1), (1, 4), (2, 3), (2, 7), (2, 11), (4, 2),
-    (7, 6), (0, 9), (6, 10), (6, 12), (8, 6), (6, 8), (1, 9), (4, 1), (2, 14), (2, 4), (3, 11), (4, 0),
-    (3, 3), (5, 2), (3, 7), (7, 12), (0, 13), (8, 12), (7, 10), (0, 15), (7, 8), (1, 13), (2, 9), (8, 10),
-    (5, 1), (3, 4), (4, 11), (1, 15), (5, 0), (8, 8), (4, 3), (3, 14), (6, 2), (4, 7), (6, 1), (2, 13),
-    (4, 4), (5, 3), (3, 9), (5, 11), (6, 0), (2, 15), (7, 2), (5, 7), (4, 14), (5, 4), (8, 2), (6, 11),
-    (3, 13), (4, 9), (7, 1), (6, 7), (8, 1), (7, 0), (6, 3), (6, 4), (3, 15), (4, 13), (8, 0), (5, 14),
-    (7, 11), (5, 9), (8, 11), (7, 7), (4, 15), (7, 3), (5, 13), (8, 7), (7, 4), (8, 3), (6, 14), (6, 9),
-    (8, 4), (5, 15), (6, 13), (7, 14), (7, 9), (6, 15), (8, 14), (8, 9), (7, 13), (8, 13), (7, 15), (8, 15),
+    (0, 12), (1, 12), (0, 5), (1, 5), (2, 12), (0, 9), (0, 11), (0, 13), (1, 9), (3, 12), (1, 11), (2, 5),
+    (1, 13), (0, 0), (4, 12), (1, 0), (2, 9), (2, 11), (3, 5), (2, 13), (5, 12), (0, 1), (0, 2), (1, 1),
+    (3, 9), (1, 2), (2, 0), (4, 5), (3, 13), (3, 11), (6, 12), (0, 4), (0, 6), (0, 7), (0, 8), (1, 4),
+    (4, 9), (4, 13), (1, 6), (2, 1), (1, 7), (2, 2), (3, 0), (1, 8), (5, 5), (7, 12), (4, 11), (0, 3),
+    (0, 10), (5, 9), (8, 12), (1, 3), (5, 13), (0, 14), (3, 1), (1, 10), (0, 15), (4, 0), (2, 4), (2, 6),
+    (1, 14), (1, 15), (3, 2), (2, 7), (2, 8), (6, 13), (5, 11), (6, 5), (6, 9), (5, 0), (3, 4), (2, 3),
+    (4, 1), (2, 10), (3, 6), (2, 14), (4, 2), (2, 15), (3, 7), (3, 8), (7, 13), (6, 11), (7, 5), (8, 13),
+    (6, 0), (8, 5), (3, 3), (4, 6), (7, 9), (3, 10), (5, 2), (4, 4), (5, 1), (8, 9), (3, 15), (4, 8),
+    (7, 11), (3, 14), (4, 7), (4, 3), (8, 11), (5, 6), (6, 1), (5, 8), (7, 0), (4, 15), (4, 14), (4, 10),
+    (5, 3), (8, 0), (6, 2), (5, 4), (6, 6), (5, 7), (5, 15), (6, 8), (5, 10), (7, 1), (5, 14), (8, 1),
+    (7, 2), (6, 3), (7, 6), (8, 2), (6, 4), (8, 6), (6, 7), (6, 14), (6, 15), (7, 8), (7, 3), (8, 8),
+    (8, 3), (7, 4), (6, 10), (7, 15), (7, 14), (8, 4), (7, 7), (8, 14), (8, 15), (8, 7), (7, 10), (8, 10),
 )
-RS_DTYPES = (BF16, BF16, F32)
+RS_DTYPES = (BF16, BF16, BF16)
 
 
 def side(pos):
@@ -84,7 +84,7 @@
     kslot = kb.at[half[2], half[0], code]
     for o in range(2):
         for k in range(LOC):
-            kslot[o * LOC + k:o * LOC + k + 1, :] = jnp.full((1, 128), keep_ref[k, o].astype(F32))
+            kslot[o * LOC + k:o * LOC + k + 1, :] = jnp.full((1, 128), keep_ref[o, k].astype(F32))
 
     barrier = pltpu.get_barrier_semaphore()
     everyone = [dev for dev, _ in group_peers] + slice_peers + [sibling]
@@ -101,10 +101,10 @@
             batch = lax.rem(q * OWN - HALO + NB + t, NB)
             remote(b3.at[batch], bg.at[t, pl.ds(pl.multiple_of(code * PB, PB), PB)], a_send.at[0], a_recv.at[t], dev).start()
 
+    for dev, q in group_peers:
+        remote(kslot, kslot, k_send.at[0], k_recv.at[0], dev).start()
     for t in arrivals:
         send_in(t)
-    for dev, q in group_peers:
-        remote(kslot, kslot, k_send.at[0], k_recv.at[0], dev).start()
 
     def own_rows(t, _):
         batch = lax.rem(first + t, NB)
@@ -392,7 +392,7 @@
         ],
         compiler_params=pltpu.CompilerParams(
             collective_id=0, has_side_effects=True, vmem_limit_bytes=62 * 1024 * 1024),
-    )(rows, eps_vir.reshape(32, 1, 128), eps_occ, domains.T, pair_keep.T)
+    )(rows, eps_vir.reshape(32, 1, 128), eps_occ, domains.T, pair_keep)
     return jnp.transpose(out.reshape(2 * NB, PB, 256), (1, 0, 2))
 
 

time: 156 us -> 130 us (0.83)
  Pallas kernels: 147 us -> 121 us
    pallas_call x1, Pallas kernels: 147 us -> 121 us  [shards(): pl.pallas_call(functools.partial(kernel, STEPS, ARRIVALS, UNITS), out_sha...]
where the time goes in v3:
time: 130 us; the launch traced here: 129 us
  Pallas kernels  121 us (93%)
  local copies, waits for them, and re-layouts  8.17 us (6%)
    pallas_call x1, Pallas kernels, shards(): pl.pallas_call(functools.partial(kernel, STEPS, ARRIVALS, UNITS), out_sha...  121 us
    reshape x1, local copies, waits for them, and re-layouts, shards(): return jnp.transpose(out.reshape(2 * NB, PB, 256), (1, 0, 2))  4.08 us
    transpose x1, local copies, waits for them, and re-layouts, shards(): rows = jnp.transpose(b_aux, (1, 0, 2)).reshape(NB, 2, PB, 256)  4.08 us

profile of v3, /device:TPU:1, one launch (start us, length us, event | category | flops | bytes accessed | tf_op | source)
XLA Modules:
  0.0 129.5 jit_solution(14893405327690858280)
XLA Ops:
  0.0 4.1 %copy.6 = bf16[64,64,256]{2,1,0:T(8,128)(2,1)} copy(bf16[64,64,256]{2,0,1:T(8,128)(2,1)} %bitcast.10) | data formatting | bytes 4194304 | tf_op jit(solution)/shard_map/transpose | solution.py:356
  4.1 121.3 %shard_map.55 = bf16[8,4,2,64,256]{4,3,2,1,0:T(8,128)(2,1)} custom-call(bf16[32,2,64,256]{3,2,1,0:T(8,128)(2,1)} %bitcast.9, f32[32,1,128]{2,1,0:T(1,128)} %bitcast.11, f32[64]{0:T(128)} %eocc_ref.1, s32[2,64]{1,0:T(2,128)} %bitcast.12, s32[2,7]{1,0:T(2,128)} %keep_ref.1), custom_call_target="tpu_custom_call" | custom-call | tf_op jit(solution)/shard_map/pallas_call | solution.py:363
  125.4 4.1 %copy.9 = bf16[64,64,256]{2,0,1:T(8,128)(2,1)} copy(bf16[64,64,256]{2,1,0:T(8,128)(2,1)} %bitcast.8) | data formatting | bytes 4194304 | tf_op jit(solution)/shard_map/reshape | solution.py:396

commit v4 on v3

--- a/solution.py
+++ b/solution.py
@@ -47,7 +47,7 @@
 
 
 def kernel(steps, arrivals, units, b_ref, evir_ref, eocc_ref, dom_ref, keep_ref, out_ref,
-           b3, bg, bt, acc, s0, r0, s1, r1, s2, r2, s3, r3, mb, mm, gam, go, rr, kb, erow, ecol,
+           raw, b3, bg, bt, acc, s0, r0, s1, r1, s2, r2, s3, r3, mb, mm, gam, go, rr, kb, erow, ecol,
            loc_sem, out_sem, a_send, a_recv, c_send, c_recv, rs_send, rs_recv, ag_send, ag_recv,
            gc_send, gc_recv, o_send, o_recv, k_send, k_recv):
     occ = lax.axis_index("occ")
@@ -78,9 +78,8 @@
         return pltpu.make_async_remote_copy(
             src_ref=src, dst_ref=dst, send_sem=send, recv_sem=recv, device_id=dev, device_id_type=MESH)
 
-    loads = [pltpu.make_async_copy(b_ref.at[:, o], b3.at[:, :, pl.ds(o * 256, 256)], loc_sem.at[o]) for o in range(2)]
-    for cp in loads:
-        cp.start()
+    load = pltpu.make_async_copy(b_ref, raw, loc_sem.at[0])
+    load.start()
     kslot = kb.at[half[2], half[0], code]
     for o in range(2):
         for k in range(LOC):
@@ -90,8 +89,17 @@
     everyone = [dev for dev, _ in group_peers] + slice_peers + [sibling]
     for dev in everyone:
         pl.semaphore_signal(barrier, inc=1, device_id=dev, device_id_type=MESH)
-    for cp in loads:
-        cp.wait()
+    load.wait()
+
+    def turn(m, _):
+        for p in range(0, PB, 32):
+            part = raw[p:p + 32, pl.ds(pl.multiple_of(m * 16, 16), 16), :].astype(F32)
+            part = jnp.swapaxes(part, 0, 1).astype(BF16)
+            for i in range(16):
+                b3[m * 8 + i // 2, p:p + 32, i % 2 * 256:i % 2 * 256 + 256] = part[i]
+        return 0
+
+    lax.fori_loop(0, 4, turn, 0)
     pl.semaphore_wait(barrier, len(everyone))
 
     first = code * OWN - HALO + NB
@@ -353,7 +361,6 @@
 
 
 def shards(b_aux, eps_occ, eps_vir, domains, pair_keep):
-    rows = jnp.transpose(b_aux, (1, 0, 2)).reshape(NB, 2, PB, 256)
     dma, vm = pltpu.SemaphoreType.DMA, pltpu.VMEM
     hbm = pl.BlockSpec(memory_space=pl.ANY)
     vmem = pl.BlockSpec(memory_space=pltpu.VMEM)
@@ -366,6 +373,7 @@
         in_specs=[hbm, vmem, smem, smem, smem],
         out_specs=hbm,
         scratch_shapes=[
+            vm((PB, 2 * NB, 256), BF16),
             vm((NB, PB, W), BF16),
             vm((LOC, PS, W), BF16),
             vm((OWN, 2, 256, PS), BF16),
@@ -392,7 +400,7 @@
         ],
         compiler_params=pltpu.CompilerParams(
             collective_id=0, has_side_effects=True, vmem_limit_bytes=62 * 1024 * 1024),
-    )(rows, eps_vir.reshape(32, 1, 128), eps_occ, domains.T, pair_keep)
+    )(b_aux, eps_vir.reshape(32, 1, 128), eps_occ, domains.T, pair_keep)
     return jnp.transpose(out.reshape(2 * NB, PB, 256), (1, 0, 2))
 
 

time: 130 us -> 126 us (0.969)
  local copies, waits for them, and re-layouts: 8.17 us -> 4.08 us
    transpose x1 -> x0, local copies, waits for them, and re-layouts: 4.08 us -> none  [shards(): rows = jnp.transpose(b_aux, (1, 0, 2)).reshape(NB, 2, PB, 256)]
where the time goes in v4:
time: 126 us
  Pallas kernels  122 us (97%)
  local copies, waits for them, and re-layouts  4.08 us (3%)
    pallas_call x1, Pallas kernels, shards(): pl.pallas_call(functools.partial(kernel, STEPS, ARRIVALS, UNITS), out_sha...  122 us
    reshape x1, local copies, waits for them, and re-layouts, shards(): return jnp.transpose(out.reshape(2 * NB, PB, 256), (1, 0, 2))  4.08 us

profile of v4, /device:TPU:1, one launch (start us, length us, event | category | flops | bytes accessed | tf_op | source)
XLA Modules:
  0.0 125.7 jit_solution(17133436473408192017)
XLA Ops:
  0.0 121.6 %shard_map.55 = bf16[8,4,2,64,256]{4,3,2,1,0:T(8,128)(2,1)} custom-call(bf16[64,64,256]{2,1,0:T(8,128)(2,1)} %b_ref.1, f32[32,1,128]{2,1,0:T(1,128)} %bitcast.7, f32[64]{0:T(128)} %eocc_ref.1, s32[2,64]{1,0:T(2,128)} %bitcast.8, s32[2,7]{1,0:T(2,128)} %keep_ref.1), custom_call_target="tpu_custom_call" | custom-call | tf_op jit(solution)/shard_map/pallas_call | solution.py:370
  121.6 4.1 %copy.8 = bf16[64,64,256]{2,0,1:T(8,128)(2,1)} copy(bf16[64,64,256]{2,1,0:T(8,128)(2,1)} %bitcast.6) | data formatting | bytes 4194304 | tf_op jit(solution)/shard_map/reshape | solution.py:404

commit v5 on v4

--- a/solution.py
+++ b/solution.py
@@ -20,24 +20,24 @@
 NCODE = 8
 PS = NCODE * PB
 SLOTS = 4
-ARRIVALS = (4, 1, 3, 0, 2, 5, 6)
+ARRIVALS = (1, 4, 3, 5, 2, 0, 6)
 UNITS = (
-    (3, 3), (3, 1), (4, 2), (6, 3), (5, 0), (4, 3), (5, 3), (5, 1),
-    (5, 2), (3, 0), (6, 1), (4, 1), (4, 0), (3, 2), (6, 0), (6, 2),
+    (3, 0), (5, 1), (6, 0), (3, 1), (3, 2), (5, 3), (6, 3), (6, 1),
+    (5, 2), (4, 3), (3, 3), (4, 1), (5, 0), (4, 2), (4, 0), (6, 2),
 )
 STEPS = (
-    (0, 12), (1, 12), (0, 5), (1, 5), (2, 12), (0, 9), (0, 11), (0, 13), (1, 9), (3, 12), (1, 11), (2, 5),
-    (1, 13), (0, 0), (4, 12), (1, 0), (2, 9), (2, 11), (3, 5), (2, 13), (5, 12), (0, 1), (0, 2), (1, 1),
-    (3, 9), (1, 2), (2, 0), (4, 5), (3, 13), (3, 11), (6, 12), (0, 4), (0, 6), (0, 7), (0, 8), (1, 4),
-    (4, 9), (4, 13), (1, 6), (2, 1), (1, 7), (2, 2), (3, 0), (1, 8), (5, 5), (7, 12), (4, 11), (0, 3),
-    (0, 10), (5, 9), (8, 12), (1, 3), (5, 13), (0, 14), (3, 1), (1, 10), (0, 15), (4, 0), (2, 4), (2, 6),
-    (1, 14), (1, 15), (3, 2), (2, 7), (2, 8), (6, 13), (5, 11), (6, 5), (6, 9), (5, 0), (3, 4), (2, 3),
-    (4, 1), (2, 10), (3, 6), (2, 14), (4, 2), (2, 15), (3, 7), (3, 8), (7, 13), (6, 11), (7, 5), (8, 13),
-    (6, 0), (8, 5), (3, 3), (4, 6), (7, 9), (3, 10), (5, 2), (4, 4), (5, 1), (8, 9), (3, 15), (4, 8),
-    (7, 11), (3, 14), (4, 7), (4, 3), (8, 11), (5, 6), (6, 1), (5, 8), (7, 0), (4, 15), (4, 14), (4, 10),
-    (5, 3), (8, 0), (6, 2), (5, 4), (6, 6), (5, 7), (5, 15), (6, 8), (5, 10), (7, 1), (5, 14), (8, 1),
-    (7, 2), (6, 3), (7, 6), (8, 2), (6, 4), (8, 6), (6, 7), (6, 14), (6, 15), (7, 8), (7, 3), (8, 8),
-    (8, 3), (7, 4), (6, 10), (7, 15), (7, 14), (8, 4), (7, 7), (8, 14), (8, 15), (8, 7), (7, 10), (8, 10),
+    (0, 14), (1, 14), (0, 4), (0, 11), (0, 9), (1, 4), (0, 0), (1, 0), (2, 14), (1, 9), (0, 1), (2, 4),
+    (1, 11), (0, 12), (1, 12), (0, 8), (2, 0), (1, 1), (0, 3), (2, 9), (1, 8), (3, 14), (0, 13), (0, 5),
+    (2, 11), (3, 4), (1, 3), (2, 12), (1, 13), (0, 10), (3, 9), (2, 1), (3, 11), (1, 10), (2, 8), (1, 5),
+    (2, 3), (4, 9), (4, 4), (3, 1), (0, 6), (2, 13), (4, 14), (4, 11), (0, 7), (2, 10), (1, 6), (0, 2),
+    (3, 8), (3, 3), (1, 7), (3, 0), (0, 15), (5, 4), (2, 5), (3, 13), (3, 10), (5, 9), (1, 2), (1, 15),
+    (4, 0), (2, 6), (4, 8), (4, 13), (4, 10), (3, 5), (4, 3), (6, 9), (3, 12), (2, 7), (6, 4), (5, 10),
+    (2, 15), (5, 8), (4, 1), (4, 5), (7, 9), (3, 6), (5, 3), (5, 13), (3, 7), (2, 2), (4, 12), (8, 9),
+    (7, 4), (6, 10), (5, 11), (4, 6), (6, 8), (5, 0), (8, 4), (5, 5), (5, 1), (6, 13), (7, 10), (3, 15),
+    (6, 3), (5, 6), (4, 7), (7, 8), (6, 5), (6, 11), (6, 0), (5, 14), (8, 10), (7, 13), (5, 12), (6, 6),
+    (7, 3), (8, 13), (6, 1), (7, 5), (3, 2), (4, 15), (8, 3), (5, 7), (8, 5), (8, 8), (7, 0), (7, 6),
+    (6, 12), (6, 14), (5, 15), (7, 1), (7, 11), (8, 0), (6, 7), (8, 6), (8, 11), (8, 1), (6, 15), (7, 12),
+    (4, 2), (7, 7), (7, 14), (8, 12), (8, 7), (7, 15), (5, 2), (8, 15), (6, 2), (8, 14), (7, 2), (8, 2),
 )
 RS_DTYPES = (BF16, BF16, BF16)
 
@@ -144,8 +144,11 @@
         ref = kb.at[half[2]]
         return remote(ref, ref, k_send.at[2], k_recv.at[2], slice_peers[2])
 
-    def order(u, n):
-        return (u + n) % 3
+    def order(u, n, h):
+        return (u + n + h) % 3
+
+    def cols(h):
+        return pl.ds(h * 256, 256)
 
     def wait_in(t):
         pltpu.make_async_copy(bg.at[0, pl.ds(0, 7 * PB)], bg.at[0, pl.ds(0, 7 * PB)], a_recv.at[t]).wait()
@@ -163,20 +166,21 @@
 
     rs_bufs = ((s1, r1), (s2, r2), (s3, r3))
 
-    def rs_copy(n, u):
+    def rs_copy(n, u, h):
         sb, rb = rs_bufs[n]
-        return remote(sb.at[u], rb.at[u], rs_send.at[n, u], rs_recv.at[n, u], slice_peers[order(u, n)])
-
-    def base_rows(u, n):
+        return remote(sb.at[u, :, cols(h)], rb.at[u, :, cols(h)], rs_send.at[n, u, h], rs_recv.at[n, u, h],
+                      slice_peers[order(u, n, h)])
+
+    def base_rows(u, n, h):
         at = core * 0
         for m in range(n):
-            at = at + half[order(u, m)] * (128 >> m)
+            at = at + half[order(u, m, h)] * (128 >> m)
         return at
 
-    def ag_copy(n, u):
+    def ag_copy(n, u, h):
         size = 128 >> n
-        ref = mb.at[u, pl.ds(pl.multiple_of(core * 256 + base_rows(u, n + 1), 32), size)]
-        return remote(ref, ref, ag_send.at[n, u], ag_recv.at[n, u], slice_peers[order(u, n)])
+        ref = mb.at[u, pl.ds(pl.multiple_of(core * 256 + base_rows(u, n + 1, h), 32), size), cols(h)]
+        return remote(ref, ref, ag_send.at[n, u, h], ag_recv.at[n, u, h], slice_peers[order(u, n, h)])
 
     def gc_copy(u):
         ref = mb.at[u, pl.ds(pl.multiple_of(core * 256, 256), 256)]
@@ -204,55 +208,62 @@
 
     def fold(n, u):
         src = r0 if n == 0 else rs_bufs[n - 1][1]
+        size = 128 >> n
+        send_to = rs_bufs[n][0]
+        step = 32
         if n == 0:
             core_copy(u).wait_recv()
-        else:
-            rs_copy(n - 1, u).wait_recv()
-        size = 128 >> n
-        near_half = half[order(u, n)]
-        base = base_rows(u, n)
-        keep_at = near_half * size
-        send_at = (1 - near_half) * size
-        send_to = rs_bufs[n][0]
-        step = 32
-
-        def far(k, _):
-            near = pl.ds(pl.multiple_of(send_at + k * step, step), step)
-            mine = pl.ds(pl.multiple_of(base + send_at + k * step, step), step)
-            val = acc[u, mine, :] + src[u, near, :].astype(F32)
-            send_to[u, pl.ds(pl.multiple_of(k * step, step), step), :] = val.astype(send_to.dtype)
-            return 0
-
-        lax.fori_loop(0, size // step, far, 0)
-        rs_copy(n, u).start()
-
-        def stay(k, _):
-            near = pl.ds(pl.multiple_of(keep_at + k * step, step), step)
-            mine = pl.ds(pl.multiple_of(base + keep_at + k * step, step), step)
-            acc[u, mine, :] = acc[u, mine, :] + src[u, near, :].astype(F32)
-            return 0
-
-        lax.fori_loop(0, size // step, stay, 0)
+        for h in range(2):
+            if n:
+                rs_copy(n - 1, u, h).wait_recv()
+            lanes = slice(h * 256, h * 256 + 256)
+            base = base_rows(u, n, h)
+            send_at = (1 - half[order(u, n, h)]) * size
+
+            def far(k, _):
+                near = pl.ds(pl.multiple_of(send_at + k * step, step), step)
+                mine = pl.ds(pl.multiple_of(base + send_at + k * step, step), step)
+                val = acc[u, mine, lanes] + src[u, near, lanes].astype(F32)
+                send_to[u, pl.ds(pl.multiple_of(k * step, step), step), lanes] = val.astype(send_to.dtype)
+                return 0
+
+            lax.fori_loop(0, size // step, far, 0)
+            rs_copy(n, u, h).start()
+        for h in range(2):
+            lanes = slice(h * 256, h * 256 + 256)
+            base = base_rows(u, n, h)
+            keep_at = half[order(u, n, h)] * size
+
+            def stay(k, _):
+                near = pl.ds(pl.multiple_of(keep_at + k * step, step), step)
+                mine = pl.ds(pl.multiple_of(base + keep_at + k * step, step), step)
+                acc[u, mine, lanes] = acc[u, mine, lanes] + src[u, near, lanes].astype(F32)
+                return 0
+
+            lax.fori_loop(0, size // step, stay, 0)
 
     def stage_amp(u):
-        rs_copy(2, u).wait_recv()
         top, s = units[u]
-        base = pl.multiple_of(base_rows(u, 3), 32)
-        rows = ecol[pl.ds(pl.multiple_of((top - HALO) * W + core * 256 + base, 32), 32), :]
-        for k in range(W // 128):
-            lanes = slice(k * 128, k * 128 + 128)
-            at = (top - s) * W + k * 128
-            total = acc[u, pl.ds(base, 32), lanes] + r3[u, :, lanes]
-            denom = rows + erow[:, at:at + 128]
-            mb[u, pl.ds(pl.multiple_of(core * 256 + base, 32), 32), lanes] = (-total / denom).astype(BF16)
-        ag_copy(2, u).start()
+        for h in range(2):
+            rs_copy(2, u, h).wait_recv()
+            base = pl.multiple_of(base_rows(u, 3, h), 32)
+            rows = ecol[pl.ds(pl.multiple_of((top - HALO) * W + core * 256 + base, 32), 32), :]
+            for k in range(2 * h, 2 * h + 2):
+                lanes = slice(k * 128, k * 128 + 128)
+                at = (top - s) * W + k * 128
+                total = acc[u, pl.ds(base, 32), lanes] + r3[u, :, lanes].astype(F32)
+                denom = rows + erow[:, at:at + 128]
+                mb[u, pl.ds(pl.multiple_of(core * 256 + base, 32), 32), lanes] = (-total / denom).astype(BF16)
+            ag_copy(2, u, h).start()
 
     def stage_ag(n, u):
-        ag_copy(n + 1, u).wait_recv()
-        ag_copy(n, u).start()
+        for h in range(2):
+            ag_copy(n + 1, u, h).wait_recv()
+            ag_copy(n, u, h).start()
 
     def stage_gc(u):
-        ag_copy(0, u).wait_recv()
+        for h in range(2):
+            ag_copy(0, u, h).wait_recv()
         gc_copy(u).start()
 
     def flag(t, orbital, offset):
@@ -332,8 +343,9 @@
             core_copy(u).wait_send()
         gc_copy(u).wait_send()
         for n in range(3):
-            rs_copy(n, u).wait_send()
-            ag_copy(n, u).wait_send()
+            for h in range(2):
+                rs_copy(n, u, h).wait_send()
+                ag_copy(n, u, h).wait_send()
 
     got, done = set(), set()
     stores = []
@@ -392,8 +404,8 @@
             vm((OWN * W, 128), F32),
             dma((2,)), dma((OWN, 2)), dma((1,)), dma((LOC,)),
             dma((n,)), dma((n,)),
-            dma((3, n)), dma((3, n)),
-            dma((3, n)), dma((3, n)),
+            dma((3, n, 2)), dma((3, n, 2)),
+            dma((3, n, 2)), dma((3, n, 2)),
             dma((n,)), dma((n,)),
             dma((1,)), dma((LOC,)),
             dma((3,)), dma((3,)),

time: 126 us -> 124 us (0.984)
  Pallas kernels: 122 us -> 120 us
    pallas_call x1, Pallas kernels: 122 us -> 120 us  [shards(): pl.pallas_call(functools.partial(kernel, STEPS, ARRIVALS, UNITS), out_sha...]
where the time goes in v5:
time: 124 us
  Pallas kernels  120 us (97%)
  local copies, waits for them, and re-layouts  4.08 us (3%)
    pallas_call x1, Pallas kernels, shards(): pl.pallas_call(functools.partial(kernel, STEPS, ARRIVALS, UNITS), out_sha...  120 us
    reshape x1, local copies, waits for them, and re-layouts, shards(): return jnp.transpose(out.reshape(2 * NB, PB, 256), (1, 0, 2))  4.08 us

profile of v5, /device:TPU:1, one launch (start us, length us, event | category | flops | bytes accessed | tf_op | source)
XLA Modules:
  0.0 124.1 jit_solution(7980884903137374144)
XLA Ops:
  0.0 120.1 %shard_map.55 = bf16[8,4,2,64,256]{4,3,2,1,0:T(8,128)(2,1)} custom-call(bf16[64,64,256]{2,1,0:T(8,128)(2,1)} %b_ref.1, f32[32,1,128]{2,1,0:T(1,128)} %bitcast.7, f32[64]{0:T(128)} %eocc_ref.1, s32[2,64]{1,0:T(2,128)} %bitcast.8, s32[2,7]{1,0:T(2,128)} %keep_ref.1), custom_call_target="tpu_custom_call" | custom-call | tf_op jit(solution)/shard_map/pallas_call | solution.py:382
  120.1 4.1 %copy.8 = bf16[64,64,256]{2,0,1:T(8,128)(2,1)} copy(bf16[64,64,256]{2,1,0:T(8,128)(2,1)} %bitcast.6) | data formatting | bytes 4194304 | tf_op jit(solution)/shard_map/reshape | solution.py:416

commit v6 on v5

--- a/solution.py
+++ b/solution.py
@@ -20,24 +20,24 @@
 NCODE = 8
 PS = NCODE * PB
 SLOTS = 4
-ARRIVALS = (1, 4, 3, 5, 2, 0, 6)
+ARRIVALS = (3, 1, 4, 0, 6, 5, 2)
 UNITS = (
-    (3, 0), (5, 1), (6, 0), (3, 1), (3, 2), (5, 3), (6, 3), (6, 1),
-    (5, 2), (4, 3), (3, 3), (4, 1), (5, 0), (4, 2), (4, 0), (6, 2),
+    (6, 1), (6, 2), (3, 0), (4, 2), (4, 3), (3, 2), (4, 0), (5, 1),
+    (6, 3), (5, 3), (6, 0), (3, 1), (4, 1), (3, 3), (5, 2), (5, 0),
 )
 STEPS = (
-    (0, 14), (1, 14), (0, 4), (0, 11), (0, 9), (1, 4), (0, 0), (1, 0), (2, 14), (1, 9), (0, 1), (2, 4),
-    (1, 11), (0, 12), (1, 12), (0, 8), (2, 0), (1, 1), (0, 3), (2, 9), (1, 8), (3, 14), (0, 13), (0, 5),
-    (2, 11), (3, 4), (1, 3), (2, 12), (1, 13), (0, 10), (3, 9), (2, 1), (3, 11), (1, 10), (2, 8), (1, 5),
-    (2, 3), (4, 9), (4, 4), (3, 1), (0, 6), (2, 13), (4, 14), (4, 11), (0, 7), (2, 10), (1, 6), (0, 2),
-    (3, 8), (3, 3), (1, 7), (3, 0), (0, 15), (5, 4), (2, 5), (3, 13), (3, 10), (5, 9), (1, 2), (1, 15),
-    (4, 0), (2, 6), (4, 8), (4, 13), (4, 10), (3, 5), (4, 3), (6, 9), (3, 12), (2, 7), (6, 4), (5, 10),
-    (2, 15), (5, 8), (4, 1), (4, 5), (7, 9), (3, 6), (5, 3), (5, 13), (3, 7), (2, 2), (4, 12), (8, 9),
-    (7, 4), (6, 10), (5, 11), (4, 6), (6, 8), (5, 0), (8, 4), (5, 5), (5, 1), (6, 13), (7, 10), (3, 15),
-    (6, 3), (5, 6), (4, 7), (7, 8), (6, 5), (6, 11), (6, 0), (5, 14), (8, 10), (7, 13), (5, 12), (6, 6),
-    (7, 3), (8, 13), (6, 1), (7, 5), (3, 2), (4, 15), (8, 3), (5, 7), (8, 5), (8, 8), (7, 0), (7, 6),
-    (6, 12), (6, 14), (5, 15), (7, 1), (7, 11), (8, 0), (6, 7), (8, 6), (8, 11), (8, 1), (6, 15), (7, 12),
-    (4, 2), (7, 7), (7, 14), (8, 12), (8, 7), (7, 15), (5, 2), (8, 15), (6, 2), (8, 14), (7, 2), (8, 2),
+    (0, 2), (1, 2), (0, 5), (2, 2), (1, 5), (0, 4), (3, 2), (0, 6), (0, 12), (2, 5), (1, 4), (1, 6),
+    (1, 12), (4, 2), (0, 13), (3, 5), (1, 13), (2, 4), (2, 6), (2, 12), (5, 2), (4, 5), (0, 1), (0, 8),
+    (0, 10), (2, 13), (1, 1), (3, 4), (1, 8), (3, 6), (1, 10), (3, 12), (6, 2), (5, 5), (0, 0), (3, 13),
+    (0, 7), (4, 4), (2, 1), (1, 0), (1, 7), (2, 8), (4, 6), (6, 5), (2, 10), (4, 12), (4, 13), (5, 4),
+    (7, 2), (0, 3), (3, 1), (2, 0), (8, 2), (1, 3), (2, 7), (5, 6), (3, 8), (7, 5), (0, 9), (3, 10),
+    (6, 4), (5, 12), (5, 13), (8, 5), (3, 0), (4, 1), (1, 9), (2, 3), (6, 6), (3, 7), (4, 8), (4, 10),
+    (7, 4), (0, 11), (6, 12), (5, 1), (6, 13), (8, 4), (4, 0), (1, 11), (2, 9), (3, 3), (7, 6), (0, 14),
+    (4, 7), (5, 8), (5, 10), (8, 6), (5, 0), (6, 1), (1, 14), (7, 12), (0, 15), (2, 11), (8, 12), (4, 3),
+    (3, 9), (7, 13), (1, 15), (5, 7), (6, 10), (6, 8), (8, 13), (6, 0), (7, 1), (3, 11), (2, 14), (5, 3),
+    (8, 1), (4, 9), (2, 15), (6, 7), (7, 10), (8, 10), (7, 0), (7, 8), (4, 11), (3, 14), (5, 9), (6, 3),
+    (8, 0), (3, 15), (8, 8), (7, 7), (5, 11), (4, 14), (6, 9), (8, 7), (4, 15), (7, 3), (6, 11), (8, 3),
+    (5, 14), (7, 9), (5, 15), (8, 9), (7, 11), (6, 14), (8, 11), (6, 15), (7, 14), (8, 14), (7, 15), (8, 15),
 )
 RS_DTYPES = (BF16, BF16, BF16)
 
@@ -78,6 +78,10 @@
         return pltpu.make_async_remote_copy(
             src_ref=src, dst_ref=dst, send_sem=send, recv_sem=recv, device_id=dev, device_id_type=MESH)
 
+    barrier = pltpu.get_barrier_semaphore()
+    everyone = [dev for dev, _ in group_peers] + slice_peers + [sibling]
+    for dev in everyone:
+        pl.semaphore_signal(barrier, inc=1, device_id=dev, device_id_type=MESH)
     load = pltpu.make_async_copy(b_ref, raw, loc_sem.at[0])
     load.start()
     kslot = kb.at[half[2], half[0], code]
@@ -85,10 +89,6 @@
         for k in range(LOC):
             kslot[o * LOC + k:o * LOC + k + 1, :] = jnp.full((1, 128), keep_ref[o, k].astype(F32))
 
-    barrier = pltpu.get_barrier_semaphore()
-    everyone = [dev for dev, _ in group_peers] + slice_peers + [sibling]
-    for dev in everyone:
-        pl.semaphore_signal(barrier, inc=1, device_id=dev, device_id_type=MESH)
     load.wait()
 
     def turn(m, _):
@@ -363,10 +363,14 @@
                     return 0
 
                 lax.fori_loop(0, NCODE, combine, 0)
-            for o in range(2):
-                cp = pltpu.make_async_copy(rr.at[:, HALO + k, :, pl.ds(o * 256, 256)], out_ref.at[:, k, o], out_sem.at[k, o])
-                cp.start()
-                stores.append(cp)
+
+    for m in range(4):
+        for p in range(0, PB, 32):
+            part = jnp.stack([rr[m * 2 + i // 8, HALO + i // 2 % 4, p:p + 32, i % 2 * 256:i % 2 * 256 + 256] for i in range(16)])
+            raw[p:p + 32, m * 16:m * 16 + 16, :] = jnp.swapaxes(part.astype(F32), 0, 1).astype(BF16)
+        cp = pltpu.make_async_copy(raw.at[:, pl.ds(m * 16, 16)], out_ref.at[:, pl.ds(m * 16, 16)], out_sem.at[m, 0])
+        cp.start()
+        stores.append(cp)
     for cp in stores:
         cp.wait()
     pltpu.make_async_copy(rr.at[pl.ds(0, 7)], rr.at[pl.ds(0, 7)], o_send.at[0]).wait()
@@ -379,9 +383,9 @@
     smem = pl.BlockSpec(memory_space=pltpu.SMEM)
     rs1, rs2, rs3 = RS_DTYPES
     n = len(UNITS)
-    out = pl.pallas_call(
+    return pl.pallas_call(
         functools.partial(kernel, STEPS, ARRIVALS, UNITS),
-        out_shape=jax.ShapeDtypeStruct((NCODE, OWN, 2, PB, 256), BF16),
+        out_shape=jax.ShapeDtypeStruct((PB, 2 * NB, 256), BF16),
         in_specs=[hbm, vmem, smem, smem, smem],
         out_specs=hbm,
         scratch_shapes=[
@@ -413,7 +417,6 @@
         compiler_params=pltpu.CompilerParams(
             collective_id=0, has_side_effects=True, vmem_limit_bytes=62 * 1024 * 1024),
     )(b_aux, eps_vir.reshape(32, 1, 128), eps_occ, domains.T, pair_keep)
-    return jnp.transpose(out.reshape(2 * NB, PB, 256), (1, 0, 2))
 
 
 def solution(mesh):

time: 124 us -> 124 us (level)
    reshape x1 -> x0, local copies, waits for them, and re-layouts: 4.08 us -> none  [shards(): return jnp.transpose(out.reshape(2 * NB, PB, 256), (1, 0, 2))]
    unnamed x0 -> x1, local copies, waits for them, and re-layouts: none -> 3.16 us
where the time goes in v6:
time: 124 us
  Pallas kernels  121 us (98%)
  local copies, waits for them, and re-layouts  3.16 us (3%)
    pallas_call x1, Pallas kernels, shards(): pl.pallas_call(functools.partial(kernel, STEPS, ARRIVALS, UNITS), out_sha...  121 us
    unnamed x1, local copies, waits for them, and re-layouts  3.16 us

profile of v6, /device:TPU:1, one launch (start us, length us, event | category | flops | bytes accessed | tf_op | source)
XLA Modules:
  0.0 124.0 jit_solution(6489635387930435656)
XLA Ops:
  0.0 120.8 %shard_map.55 = bf16[64,64,256]{2,1,0:T(8,128)(2,1)} custom-call(bf16[64,64,256]{2,1,0:T(8,128)(2,1)} %b_ref.1, f32[32,1,128]{2,1,0:T(1,128)} %bitcast.2, f32[64]{0:T(128)} %eocc_ref.1, s32[2,64]{1,0:T(2,128)} %bitcast.3, s32[2,7]{1,0:T(2,128)} %keep_ref.1), custom_call_target="tpu_custom_call" | custom-call | tf_op jit(solution)/shard_map/pallas_call | solution.py:386
  120.8 3.2 %copy.7 = bf16[64,64,256]{2,1,0:T(8,128)(2,1)} copy(bf16[64,64,256]{2,1,0:T(8,128)(2,1)} %shard_map.55) | data formatting | bytes 4194304

commit v7 on v6

--- a/solution.py
+++ b/solution.py
@@ -182,6 +182,10 @@
         ref = mb.at[u, pl.ds(pl.multiple_of(core * 256 + base_rows(u, n + 1, h), 32), size), cols(h)]
         return remote(ref, ref, ag_send.at[n, u, h], ag_recv.at[n, u, h], slice_peers[order(u, n, h)])
 
+    def ag_piece(n, u, h, at, size):
+        ref = mb.at[u, pl.ds(pl.multiple_of(core * 256 + at, 32), size), cols(h)]
+        remote(ref, ref, ag_send.at[n, u, h], ag_recv.at[n, u, h], slice_peers[order(u, n, h)]).start()
+
     def gc_copy(u):
         ref = mb.at[u, pl.ds(pl.multiple_of(core * 256, 256), 256)]
         return remote(ref, ref, gc_send.at[u], gc_recv.at[u], sibling)
@@ -254,12 +258,16 @@
                 total = acc[u, pl.ds(base, 32), lanes] + r3[u, :, lanes].astype(F32)
                 denom = rows + erow[:, at:at + 128]
                 mb[u, pl.ds(pl.multiple_of(core * 256 + base, 32), 32), lanes] = (-total / denom).astype(BF16)
-            ag_copy(2, u, h).start()
+            for n in (2, 1, 0):
+                ag_piece(n, u, h, base_rows(u, 3, h), 32)
 
     def stage_ag(n, u):
         for h in range(2):
             ag_copy(n + 1, u, h).wait_recv()
-            ag_copy(n, u, h).start()
+            size = 64 >> n
+            at = base_rows(u, n + 1, h) + (1 - half[order(u, n + 1, h)]) * size
+            for m in range(n, -1, -1):
+                ag_piece(m, u, h, at, size)
 
     def stage_gc(u):
         for h in range(2):

time: 124 us -> 124 us (level)
  no operation moved by 1% of the time
where the time goes in v7:
time: 124 us
  Pallas kernels  121 us (98%)
  local copies, waits for them, and re-layouts  3.16 us (3%)
    pallas_call x1, Pallas kernels, shards(): pl.pallas_call(functools.partial(kernel, STEPS, ARRIVALS, UNITS), out_sha...  121 us
    unnamed x1, local copies, waits for them, and re-layouts  3.16 us

profile of v7, /device:TPU:1, one launch (start us, length us, event | category | flops | bytes accessed | tf_op | source)
XLA Modules:
  0.0 123.9 jit_solution(4948078475656659373)
XLA Ops:
  0.0 120.7 %shard_map.55 = bf16[64,64,256]{2,1,0:T(8,128)(2,1)} custom-call(bf16[64,64,256]{2,1,0:T(8,128)(2,1)} %b_ref.1, f32[32,1,128]{2,1,0:T(1,128)} %bitcast.2, f32[64]{0:T(128)} %eocc_ref.1, s32[2,64]{1,0:T(2,128)} %bitcast.3, s32[2,7]{1,0:T(2,128)} %keep_ref.1), custom_call_target="tpu_custom_call" | custom-call | tf_op jit(solution)/shard_map/pallas_call | solution.py:394
  120.8 3.2 %copy.7 = bf16[64,64,256]{2,1,0:T(8,128)(2,1)} copy(bf16[64,64,256]{2,1,0:T(8,128)(2,1)} %shard_map.55) | data formatting | bytes 4194304
